TPU v7x, 256 devices: a whole 4x4x8 slice. The times are simulated.
256 devices in a mesh: grp: 4 (over z_hi), dev: 64 (over y, z_lo, x, core).
Axes of the slice: x: 4, y: 4, z: 8 (z_hi: 4, z_lo: 2; z = z_hi * 2 + z_lo), core: 2. Of those that a mesh axis runs over, the one named last changes fastest.
Arguments:
- adjoint: float32 [16, 8, 512, 8, 128], P('grp', None, 'dev'), may hold values from -6 to 6
- right_side: float32 [16, 8, 512, 8, 128], P('grp', None, 'dev'), may hold values from -6 to 6
- velocity: float32 [3, 16, 8, 512, 8, 128], P(None, 'grp', None, 'dev'), may hold values from -1.2 to 1.2
- conductivity: float32 [16, 8, 512, 8, 128], P('grp', None, 'dev'), may hold values from 0.002 to 0.02
- mass_term: float32 [16, 8, 512, 8, 128], P('grp', None, 'dev'), may hold values from 0.5 to 2
- fdm_inverse: float32 [16, 8, 512, 8, 128], P('grp', None, 'dev'), may hold values from 0.05 to 1
- coarse_factor: float32 [8192, 8192], P(('grp', 'dev')), may hold values from -0.5 to 0.5
Outputs:
- residual: float32 [16, 8, 512, 8, 128], P('grp', None, 'dev')
- correction: float32 [16, 8, 512, 8, 128], P('grp', None, 'dev')
All inputs are finite; a program needn't handle non-finite values.
Results may differ from a plain program's by a relative error of at most 0.0003.
Values sent between devices are 32-bit elements; how exact they have to be, the bound alone decides.
A program may use at most 64 MiB of HBM per device.

v0:
```python
import math

import jax
import jax.numpy as jnp
from jax import lax
from jax.sharding import PartitionSpec as P

GLL_POINTS = [
    -1.0,
    -0.871740148509607,
    -0.591700181433142,
    -0.209299217902479,
    0.209299217902479,
    0.591700181433142,
    0.871740148509607,
    1.0,
]
HIGHEST_PRECISION = lax.Precision.HIGHEST


def extended(cells, sides, width):
    for axis, dim in sides:
        count = lax.axis_size(axis)
        ends = count - 1
        head = lax.slice_in_dim(cells, 0, width, axis=dim)
        tail = lax.slice_in_dim(cells, cells.shape[dim] - width, cells.shape[dim], axis=dim)
        cells = jnp.concatenate(
            [
                lax.ppermute(tail, axis, [(i, (i + 1) % count) for i in range(ends)]),
                cells,
                lax.ppermute(head, axis, [((i + 1) % count, i) for i in range(ends)]),
            ],
            axis=dim,
        )
    return cells


def legendre_value(point, highest):
    previous = 1.0
    current = point
    for degree in range(1, highest):
        previous, current = (
            current,
            ((2 * degree + 1) * point * current - degree * previous) / (degree + 1),
        )
    return current


def identity_list(dimension):
    return [
        [1.0 if row_index == col_index else 0.0 for col_index in range(dimension)]
        for row_index in range(dimension)
    ]


def transpose_list(matrix):
    return [
        [matrix[row_index][col_index] for row_index in range(len(matrix))]
        for col_index in range(len(matrix[0]))
    ]


def matrix_product(left, right):
    inner_size = len(right)
    return [
        [
            sum((left[row_index][inner] * right[inner][col_index] for inner in range(inner_size)))
            for col_index in range(len(right[0]))
        ]
        for row_index in range(len(left))
    ]


def jacobi_eigen(matrix):
    current = [list(line) for line in matrix]
    dimension = len(matrix)
    rotations = identity_list(dimension)
    for repeat in range(12):
        for row_index in range(dimension - 1):
            for col_index in range(row_index + 1, dimension):
                angle = 0.5 * math.atan2(
                    2.0 * current[row_index][col_index],
                    current[row_index][row_index] - current[col_index][col_index],
                )
                cosine = math.cos(angle)
                sine_value = math.sin(angle)
                rotation = identity_list(dimension)
                rotation[row_index][row_index] = cosine
                rotation[col_index][col_index] = cosine
                rotation[row_index][col_index] = -sine_value
                rotation[col_index][row_index] = sine_value
                current = matrix_product(
                    matrix_product(transpose_list(rotation), current), rotation
                )
                rotations = matrix_product(rotations, rotation)
    ordering = sorted(range(dimension), key=lambda position: current[position][position])
    return [
        [rotations[row_index][position] for position in ordering] for row_index in range(dimension)
    ]


def element_tables():
    total_points = len(GLL_POINTS)
    weights_bary = []
    for row_index in range(total_points):
        product_value = 1.0
        for col_index in range(total_points):
            if col_index != row_index:
                product_value = product_value * (GLL_POINTS[row_index] - GLL_POINTS[col_index])
        weights_bary.append(1.0 / product_value)
    derivative = [[0.0] * total_points for row_index in range(total_points)]
    for row_index in range(total_points):
        for col_index in range(total_points):
            if col_index != row_index:
                derivative[row_index][col_index] = (
                    weights_bary[col_index]
                    / weights_bary[row_index]
                    / (GLL_POINTS[row_index] - GLL_POINTS[col_index])
                )
        derivative[row_index][row_index] = -sum(derivative[row_index])
    quadrature = [
        2.0 / ((total_points - 1) * total_points * legendre_value(point, total_points - 1) ** 2)
        for point in GLL_POINTS
    ]
    stiffness = [
        [
            sum(
                (
                    derivative[inner][row_index] * quadrature[inner] * derivative[inner][col_index]
                    for inner in range(total_points)
                )
            )
            + (quadrature[row_index] if row_index == col_index else 0.0)
            for col_index in range(total_points)
        ]
        for row_index in range(total_points)
    ]
    return (derivative, jacobi_eigen(stiffness))


def block_diagonal(blocks, matrix):
    node_count = len(matrix)
    total = blocks * node_count
    return [
        [
            (
                matrix[row_index % node_count][col_index % node_count]
                if row_index // node_count == col_index // node_count
                else 0.0
            )
            for col_index in range(total)
        ]
        for row_index in range(total)
    ]


def assembly_table(blocks, node_count):
    total = blocks * node_count
    shared_index = [
        position // node_count * (node_count - 1) + position % node_count
        for position in range(total)
    ]
    return [
        [
            1.0 if shared_index[row_index] == shared_index[col_index] else 0.0
            for col_index in range(total)
        ]
        for row_index in range(total)
    ]


def along_first(matrix, field):
    return jnp.einsum("ai,xiyjz->xayjz", matrix, field, precision=HIGHEST_PRECISION)


def along_second(matrix, field):
    return jnp.einsum("bj,xiyjz->xiybz", matrix, field, precision=HIGHEST_PRECISION)


def along_third(field, table):
    return jnp.einsum("xiyjz,zw->xiyjw", field, table, precision=HIGHEST_PRECISION)


def to_grid(field, axis_elem):
    elements = field.shape[axis_elem]
    node_count = field.shape[axis_elem + 1]
    lower_face = lax.index_in_dim(field, 0, axis_elem + 1, keepdims=False)
    upper_face = lax.index_in_dim(field, node_count - 1, axis_elem + 1, keepdims=False)
    interior = lax.slice_in_dim(field, 1, node_count - 1, axis=axis_elem + 1)
    joints = jnp.concatenate(
        [
            lax.slice_in_dim(lower_face, 0, 1, axis=axis_elem),
            lax.slice_in_dim(upper_face, 0, elements - 1, axis=axis_elem)
            + lax.slice_in_dim(lower_face, 1, elements, axis=axis_elem),
            lax.slice_in_dim(upper_face, elements - 1, elements, axis=axis_elem),
        ],
        axis=axis_elem,
    )
    leading = jnp.concatenate(
        [
            jnp.expand_dims(lax.slice_in_dim(joints, 0, elements, axis=axis_elem), axis_elem + 1),
            interior,
        ],
        axis=axis_elem + 1,
    )
    new_shape = (
        leading.shape[:axis_elem] + (elements * (node_count - 1),) + leading.shape[axis_elem + 2 :]
    )
    merged = leading.reshape(new_shape)
    return jnp.concatenate(
        [merged, lax.slice_in_dim(joints, elements, elements + 1, axis=axis_elem)], axis=axis_elem
    )


def from_grid(grid, axis_elem, elements, node_count):
    span = elements * (node_count - 1)
    leading = lax.slice_in_dim(grid, 0, span, axis=axis_elem)
    split_shape = (
        leading.shape[:axis_elem] + (elements, node_count - 1) + leading.shape[axis_elem + 1 :]
    )
    leading = leading.reshape(split_shape)
    trailing = lax.slice_in_dim(
        grid, node_count - 1, span + 1, stride=node_count - 1, axis=axis_elem
    )
    return jnp.concatenate([leading, jnp.expand_dims(trailing, axis_elem + 1)], axis=axis_elem + 1)


def add_rims(padded, axis_index):
    length = padded.shape[axis_index]
    interior = lax.slice_in_dim(padded, 1, length - 1, axis=axis_index)
    before = lax.slice_in_dim(padded, 0, 1, axis=axis_index)
    beyond = lax.slice_in_dim(padded, length - 1, length, axis=axis_index)
    leading = lax.slice_in_dim(interior, 0, 1, axis=axis_index) + before
    trailing = lax.slice_in_dim(interior, length - 3, length - 2, axis=axis_index) + beyond
    middle = lax.slice_in_dim(interior, 1, length - 3, axis=axis_index)
    return jnp.concatenate([leading, middle, trailing], axis=axis_index)


def assemble(field, z_table):
    field = along_third(field, z_table)
    elements_first = field.shape[0]
    elements_second = field.shape[2]
    node_count = field.shape[1]
    grid = to_grid(to_grid(field, 0), 1)
    padded_first = extended(grid, (("grp", 0),), 1)
    partial_grid = add_rims(padded_first, 0)
    padded_second = extended(partial_grid, (("dev", 1),), 1)
    summed = add_rims(padded_second, 1)
    return from_grid(
        from_grid(summed, 1, elements_second, node_count), 0, elements_first, node_count
    )


def body(adjoint, right_side, velocity, conductivity, mass_term, fdm_inverse, coarse_factor):
    derivative, eigen_vectors = element_tables()
    node_count = adjoint.shape[1]
    blocks = adjoint.shape[4] // node_count
    derivative_table = jnp.asarray(derivative, jnp.float32)
    vectors_table = jnp.asarray(eigen_vectors, jnp.float32)
    backward_list = block_diagonal(blocks, derivative)
    vectors_list = block_diagonal(blocks, eigen_vectors)
    forward_z = jnp.asarray(transpose_list(backward_list), jnp.float32)
    backward_z = jnp.asarray(backward_list, jnp.float32)
    spectral_z = jnp.asarray(vectors_list, jnp.float32)
    physical_z = jnp.asarray(transpose_list(vectors_list), jnp.float32)
    z_table = jnp.asarray(assembly_table(blocks, node_count), jnp.float32)
    flux_first = conductivity * along_first(derivative_table, adjoint) + velocity[0] * adjoint
    flux_second = conductivity * along_second(derivative_table, adjoint) + velocity[1] * adjoint
    flux_third = conductivity * along_third(adjoint, forward_z) + velocity[2] * adjoint
    local = (
        mass_term * adjoint
        + along_first(derivative_table.T, flux_first)
        + along_second(derivative_table.T, flux_second)
        + along_third(flux_third, backward_z)
    )
    residual = right_side - assemble(local, z_table)
    column_means = jnp.sum(residual, axis=(1, 3, 4)) / float(
        node_count * node_count * adjoint.shape[4]
    )
    partial_inner = jnp.dot(column_means.reshape(-1), coarse_factor, precision=HIGHEST_PRECISION)
    inner_vector = lax.psum(partial_inner, ("grp", "dev"))
    coarse_values = jnp.dot(coarse_factor, inner_vector, precision=HIGHEST_PRECISION)
    coarse_field = coarse_values.reshape(adjoint.shape[0], adjoint.shape[2])
    spectral = along_third(
        along_second(vectors_table.T, along_first(vectors_table.T, residual)), spectral_z
    )
    spectral = fdm_inverse * spectral
    local_solve = along_third(
        along_second(vectors_table, along_first(vectors_table, spectral)), physical_z
    )
    combined = local_solve + coarse_field[:, None, :, None, None]
    correction = assemble(combined, z_table)
    return (residual, correction)


def solution(mesh):
    in_specs = (
        P("grp", None, "dev", None, None),
        P("grp", None, "dev", None, None),
        P(None, "grp", None, "dev", None, None),
        P("grp", None, "dev", None, None),
        P("grp", None, "dev", None, None),
        P("grp", None, "dev", None, None),
        P(("grp", "dev"), None),
    )
    out_specs = (P("grp", None, "dev", None, None), P("grp", None, "dev", None, None))
    return jax.shard_map(body, mesh=mesh, in_specs=in_specs, out_specs=out_specs, check_vma=False)
```

profile of v0, /device:TPU:71, one launch (start us, length us, event | category | flops | bytes accessed | tf_op | source)
XLA Modules:
  0.0 161.9 jit_solution(5436711741309406669)
XLA Ops:
  0.7 3.5 %fusion.3 = f32[4,8,8,8,128]{4,3,2,1,0:T(8,128)S(1)} fusion(f32[4,8,8,8,128]{4,3,2,1,0:T(8,128)} %param.17, f32[8,8,1,1,1]{1,0,4,3,2:T(8,128)} %constant.33, f32[4,8,8,8,128]{4,3,2,1,0:T(8,128)} %param.14, f32[3,4,8,8,8,128]{5,4,3,2,1,0:T(8,128)} %param.16), kind=kOutput, calls=%fused_computation.18 | convolution fusion | flops 25952256 | bytes 5246976 | tf_op jit(solution)/shard_map/bj,xiyjz->xiybz/dot_general | solution.py:177
  4.3 3.1 %fusion.7 = f32[4,8,8,8,128]{4,1,3,2,0:T(8,128)S(1)} fusion(f32[8,8,1,1,1]{1,0,4,3,2:T(8,128)S(1)} %copy-done.13, f32[1,4,8,8,8,128]{5,4,3,2,1,0:T(8,128)S(1)} %slice-done, f32[4,8,8,8,128]{4,3,2,1,0:T(8,128)S(1)} %copy-done.2, f32[4,8,8,8,128]{4,3,2,1,0:T(8,128)S(1)} %copy-done.1), kind=kOutput, calls=%fused_computation.24 | convolution fusion | flops 25952256 | bytes 4194560 | tf_op jit(solution)/shard_map/ai,xiyjz->xayjz/dot_general | solution.py:173
  7.4 1.0 fusion.35
  8.5 1.0 fusion.1
  9.5 2.6 %fusion.5 = f32[4,8,8,8,128]{4,1,3,2,0:T(8,128)S(1)} fusion(f32[4,8,8,8,128]{4,1,3,2,0:T(8,128)S(1)} %fusion.7, f32[8,8,1,1,1]{1,0,4,3,2:T(8,128)S(1)} %copy-done.13, f32[4,8,8,128,8]{3,4,2,1,0:T(8,128)S(1)} %fusion.35, f32[4,8,8,8,128]{4,3,2,1,0:T(8,128)S(1)} %copy-done.6, f32[4,8,8,8,128]{4,3,2,1,0:T(8,128)S(1)} %copy-done.1), kind=kOutput, calls=%fused_computation.21 | convolution fusion | flops 25952256 | bytes 5243136 | tf_op jit(solution)/shard_map/ai,xiyjz->xayjz/dot_general | solution.py:173
  12.2 1.4 convolution_add_fusion.1
  13.7 1.0 fusion.16
  16.0 6.1 %collective-permute-start = (f32[1,57,128]{2,0,1:T(1,128)S(1)}, f32[1,57,128]{2,0,1:T(1,128)S(1)}, u32[]{:S(2)}, u32[]{:S(2)}) collective-permute-start(f32[1,57,128]{2,0,1:T(1,128)S(1)} %pad_maximum_fusion.11), channel_id=1, source_target_pairs={{0,64},{64,128},{128,192},{1,65},{65,129},{129,193},{2,66},{66,130... | collective-permute-start | bytes 87560 | tf_op jit(solution)/shard_map/ppermute | solution.py:29
  22.1 1.0 collective-permute-done
  23.1 1.9 %collective-permute-start.1 = (f32[1,57,128]{2,0,1:T(1,128)S(1)}, f32[1,57,128]{2,0,1:T(1,128)S(1)}, u32[]{:S(2)}, u32[]{:S(2)}) collective-permute-start(f32[1,57,128]{2,0,1:T(1,128)S(1)} %get-tuple-element.7), channel_id=1, source_target_pairs={{64,0},{128,64},{192,128},{65,1},{129,65},{193,129},{66,2},{130,66... | collective-permute-start | bytes 87560 | tf_op jit(solution)/shard_map/ppermute | solution.py:31
  25.0 5.1 %collective-permute-done.1 = f32[1,57,128]{2,0,1:T(1,128)S(1)} collective-permute-done((f32[1,57,128]{2,0,1:T(1,128)S(1)}, f32[1,57,128]{2,0,1:T(1,128)S(1)}, u32[]{:S(2)}, u32[]{:S(2)}) %collective-permute-start.1) | collective-permute-done | bytes 29216 | tf_op jit(solution)/shard_map/ppermute | solution.py:31
  30.3 5.1 %collective-permute-start.2 = (f32[29,1,128]{2,0,1:T(8,128)S(1)}, f32[29,1,128]{2,0,1:T(8,128)S(1)}, u32[]{:S(2)}, u32[]{:S(2)}) collective-permute-start(f32[29,1,128]{2,0,1:T(8,128)S(1)} %get-tuple-element.22), channel_id=1, source_target_pairs={{0,1},{1,2},{2,3},{3,4},{4,5},{5,6},{6,7},{7,8},{8,9},{9,10},{10,1... | collective-permute-start | bytes 44552 | tf_op jit(solution)/shard_map/ppermute | solution.py:29
  35.5 1.9 %collective-permute-start.3 = (f32[29,1,128]{2,0,1:T(8,128)S(1)}, f32[29,1,128]{2,0,1:T(8,128)S(1)}, u32[]{:S(2)}, u32[]{:S(2)}) collective-permute-start(f32[29,1,128]{2,0,1:T(8,128)S(1)} %get-tuple-element.23), channel_id=1, source_target_pairs={{1,0},{2,1},{3,2},{4,3},{5,4},{6,5},{7,6},{8,7},{9,8},{10,9},{11,1... | collective-permute-start | bytes 44552 | tf_op jit(solution)/shard_map/ppermute | solution.py:31
  37.5 5.2 %collective-permute-done.3 = f32[29,1,128]{2,0,1:T(8,128)S(1)} collective-permute-done((f32[29,1,128]{2,0,1:T(8,128)S(1)}, f32[29,1,128]{2,0,1:T(8,128)S(1)}, u32[]{:S(2)}, u32[]{:S(2)}) %collective-permute-start.3) | collective-permute-done | bytes 14880 | tf_op jit(solution)/shard_map/ppermute | solution.py:31
  43.9 1.6 fusion.31
  45.5 1.6 %convolution_bitcast_fusion.3 = f32[4,8,8,8,128]{4,1,3,2,0:T(8,128)S(1)} fusion(f32[8,8,1,1,1]{0,1,4,3,2:T(8,128)S(1)} %copy-done.9, f32[4,8,8,8,128]{4,3,2,1,0:T(8,128)S(1)} %get-tuple-element.5), kind=kOutput, calls=%fused_computation.11 | convolution fusion | flops 25165824 | bytes 2097408 | tf_op jit(solution)/shard_map/ai,xiyjz->xayjz/dot_general | solution.py:173
  47.1 1.1 convolution_bitcast_fusion.2
  48.2 1.0 convolution_multiply_fusion
  49.2 1.6 convolution_bitcast_fusion.1
  50.8 1.1 convolution_bitcast_fusion
  52.6 74.8 %psum.7 = f32[8192]{0:T(1024)S(1)} all-reduce(f32[8192]{0:T(1024)S(1)} %bitcast.184), channel_id=1, replica_groups=mesh['grp'=4,'dev'=64] {'grp','dev'}, use_global_device_ids=true, to_apply=%region_1.0 | all-reduce | flops 8192 | bytes 65536 | tf_op jit(solution)/shard_map/psum | solution.py:281
  127.4 0.9 convolution_bitcast_fusion.8
  128.4 1.0 convolution_add_fusion
  129.4 1.0 fusion.37
  131.6 5.5 %collective-permute-start.4 = (f32[1,57,128]{2,0,1:T(1,128)S(1)}, f32[1,57,128]{2,0,1:T(1,128)S(1)}, u32[]{:S(2)}, u32[]{:S(2)}) collective-permute-start(f32[1,57,128]{2,0,1:T(1,128)S(1)} %pad_maximum_fusion.9), channel_id=1, source_target_pairs={{0,64},{64,128},{128,192},{1,65},{65,129},{129,193},{2,66},{66,130... | collective-permute-start | bytes 87560 | tf_op jit(solution)/shard_map/ppermute | solution.py:29
  137.1 1.0 collective-permute-done.4
  138.1 1.9 %collective-permute-start.5 = (f32[1,57,128]{2,0,1:T(1,128)S(1)}, f32[1,57,128]{2,0,1:T(1,128)S(1)}, u32[]{:S(2)}, u32[]{:S(2)}) collective-permute-start(f32[1,57,128]{2,0,1:T(1,128)S(1)} %get-tuple-element.3), channel_id=1, source_target_pairs={{64,0},{128,64},{192,128},{65,1},{129,65},{193,129},{66,2},{130,66... | collective-permute-start | bytes 87560 | tf_op jit(solution)/shard_map/ppermute | solution.py:31
  140.0 5.5 %collective-permute-done.5 = f32[1,57,128]{2,0,1:T(1,128)S(1)} collective-permute-done((f32[1,57,128]{2,0,1:T(1,128)S(1)}, f32[1,57,128]{2,0,1:T(1,128)S(1)}, u32[]{:S(2)}, u32[]{:S(2)}) %collective-permute-start.5) | collective-permute-done | bytes 29216 | tf_op jit(solution)/shard_map/ppermute | solution.py:31
  145.7 6.7 %collective-permute-start.6 = (f32[29,1,128]{2,0,1:T(8,128)S(1)}, f32[29,1,128]{2,0,1:T(8,128)S(1)}, u32[]{:S(2)}, u32[]{:S(2)}) collective-permute-start(f32[29,1,128]{2,0,1:T(8,128)S(1)} %get-tuple-element.18), channel_id=1, source_target_pairs={{0,1},{1,2},{2,3},{3,4},{4,5},{5,6},{6,7},{7,8},{8,9},{9,10},{10,1... | collective-permute-start | bytes 44552 | tf_op jit(solution)/shard_map/ppermute | solution.py:29
  152.4 1.9 %collective-permute-start.7 = (f32[29,1,128]{2,0,1:T(8,128)S(1)}, f32[29,1,128]{2,0,1:T(8,128)S(1)}, u32[]{:S(2)}, u32[]{:S(2)}) collective-permute-start(f32[29,1,128]{2,0,1:T(8,128)S(1)} %get-tuple-element.19), channel_id=1, source_target_pairs={{1,0},{2,1},{3,2},{4,3},{5,4},{6,5},{7,6},{8,7},{9,8},{10,9},{11,1... | collective-permute-start | bytes 44552 | tf_op jit(solution)/shard_map/ppermute | solution.py:31
  154.4 5.2 %collective-permute-done.7 = f32[29,1,128]{2,0,1:T(8,128)S(1)} collective-permute-done((f32[29,1,128]{2,0,1:T(8,128)S(1)}, f32[29,1,128]{2,0,1:T(8,128)S(1)}, u32[]{:S(2)}, u32[]{:S(2)}) %collective-permute-start.7) | collective-permute-done | bytes 14880 | tf_op jit(solution)/shard_map/ppermute | solution.py:31
  160.8 1.1 pad_maximum_fusion.2
  (94 shorter events, 6.1 us)
Async XLA Ops:
  0.6 51.4 %copy-start = (f32[32,8192]{1,0:T(8,128)S(1)}, f32[32,8192]{1,0:T(8,128)}, u32[]{:S(2)}) copy-start(f32[32,8192]{1,0:T(8,128)} %param.20) | copy-start | bytes 3145732
  0.6 3.6 %copy-start.13 = (f32[8,8,1,1,1]{1,0,4,3,2:T(8,128)S(1)}, f32[8,8,1,1,1]{1,0,4,3,2:T(8,128)}, u32[]{:S(2)}) copy-start(f32[8,8,1,1,1]{1,0,4,3,2:T(8,128)} %constant.33) | copy-start | bytes 772
  0.7 3.6 %slice-start = ((f32[3,4,8,8,8,128]{5,4,3,2,1,0:T(8,128)}), f32[1,4,8,8,8,128]{5,4,3,2,1,0:T(8,128)S(1)}, s32[]{:S(2)}) async-start(f32[3,4,8,8,8,128]{5,4,3,2,1,0:T(8,128)} %param.16), calls=%async_computation | async-start | bytes 2097152 | tf_op jit(solution)/shard_map/slice | solution.py:267
  0.7 3.6 %copy-start.2 = (f32[4,8,8,8,128]{4,3,2,1,0:T(8,128)S(1)}, f32[4,8,8,8,128]{4,3,2,1,0:T(8,128)}, u32[]{:S(2)}) copy-start(f32[4,8,8,8,128]{4,3,2,1,0:T(8,128)} %param.17) | copy-start | bytes 3145732
  0.7 3.6 %copy-start.1 = (f32[4,8,8,8,128]{4,3,2,1,0:T(8,128)S(1)}, f32[4,8,8,8,128]{4,3,2,1,0:T(8,128)}, u32[]{:S(2)}) copy-start(f32[4,8,8,8,128]{4,3,2,1,0:T(8,128)} %param.14) | copy-start | bytes 3145732
  4.3 4.2 %copy-start.3 = (f32[3,4,8,8,8,128]{5,4,3,2,1,0:T(8,128)S(1)}, f32[3,4,8,8,8,128]{5,4,3,2,1,0:T(8,128)}, u32[]{:S(2)}) copy-start(f32[3,4,8,8,8,128]{5,4,3,2,1,0:T(8,128)} %param.16) | copy-start | bytes 9437188
  4.3 4.2 %copy-start.8 = (f32[128,128,1,1,1]{1,0,4,3,2:T(8,128)S(1)}, f32[128,128,1,1,1]{1,0,4,3,2:T(8,128)}, u32[]{:S(2)}) copy-start(f32[128,128,1,1,1]{1,0,4,3,2:T(8,128)} %constant.34) | copy-start | bytes 196612
  7.4 2.1 %copy-start.6 = (f32[4,8,8,8,128]{4,3,2,1,0:T(8,128)S(1)}, f32[4,8,8,8,128]{4,3,2,1,0:T(8,128)}, u32[]{:S(2)}) copy-start(f32[4,8,8,8,128]{4,3,2,1,0:T(8,128)} %param.18) | copy-start | bytes 3145732
  9.5 2.7 %copy-start.12 = (f32[128,128,1,1,1]{1,0,4,3,2:T(8,128)S(1)}, f32[128,128,1,1,1]{1,0,4,3,2:T(8,128)}, u32[]{:S(2)}) copy-start(f32[128,128,1,1,1]{1,0,4,3,2:T(8,128)} %constant.35) | copy-start | bytes 196612
  9.5 4.1 %copy-start.7 = (f32[128,128,1,1,1]{1,0,4,3,2:T(8,128)S(1)}, f32[128,128,1,1,1]{1,0,4,3,2:T(8,128)}, u32[]{:S(2)}) copy-start(f32[128,128,1,1,1]{1,0,4,3,2:T(8,128)} %constant.36) | copy-start | bytes 196612
  16.0 7.1 %collective-permute-start = (f32[1,57,128]{2,0,1:T(1,128)S(1)}, f32[1,57,128]{2,0,1:T(1,128)S(1)}, u32[]{:S(2)}, u32[]{:S(2)}) collective-permute-start(f32[1,57,128]{2,0,1:T(1,128)S(1)} %pad_maximum_fusion.11), channel_id=1, source_target_pairs={{0,64},{64,128},{128,192},{1,65},{65,129},{129,193},{2,66},{66,130... | collective-permute-start | bytes 87560 | tf_op jit(solution)/shard_map/ppermute | solution.py:29
  23.1 7.0 %collective-permute-start.1 = (f32[1,57,128]{2,0,1:T(1,128)S(1)}, f32[1,57,128]{2,0,1:T(1,128)S(1)}, u32[]{:S(2)}, u32[]{:S(2)}) collective-permute-start(f32[1,57,128]{2,0,1:T(1,128)S(1)} %get-tuple-element.7), channel_id=1, source_target_pairs={{64,0},{128,64},{192,128},{65,1},{129,65},{193,129},{66,2},{130,66... | collective-permute-start | bytes 87560 | tf_op jit(solution)/shard_map/ppermute | solution.py:31
  30.3 7.2 %collective-permute-start.2 = (f32[29,1,128]{2,0,1:T(8,128)S(1)}, f32[29,1,128]{2,0,1:T(8,128)S(1)}, u32[]{:S(2)}, u32[]{:S(2)}) collective-permute-start(f32[29,1,128]{2,0,1:T(8,128)S(1)} %get-tuple-element.22), channel_id=1, source_target_pairs={{0,1},{1,2},{2,3},{3,4},{4,5},{5,6},{6,7},{7,8},{8,9},{9,10},{10,1... | collective-permute-start | bytes 44552 | tf_op jit(solution)/shard_map/ppermute | solution.py:29
  35.5 7.2 %collective-permute-start.3 = (f32[29,1,128]{2,0,1:T(8,128)S(1)}, f32[29,1,128]{2,0,1:T(8,128)S(1)}, u32[]{:S(2)}, u32[]{:S(2)}) collective-permute-start(f32[29,1,128]{2,0,1:T(8,128)S(1)} %get-tuple-element.23), channel_id=1, source_target_pairs={{1,0},{2,1},{3,2},{4,3},{5,4},{6,5},{7,6},{8,7},{9,8},{10,9},{11,1... | collective-permute-start | bytes 44552 | tf_op jit(solution)/shard_map/ppermute | solution.py:31
  43.0 2.5 %copy-start.9 = (f32[8,8,1,1,1]{0,1,4,3,2:T(8,128)S(1)}, f32[8,8,1,1,1]{0,1,4,3,2:T(8,128)}, u32[]{:S(2)}) copy-start(f32[8,8,1,1,1]{0,1,4,3,2:T(8,128)} %constant.37) | copy-start | bytes 772
  43.9 4.3 %copy-start.5 = (f32[4,8,8,8,128]{4,3,2,1,0:T(8,128)S(1)}, f32[4,8,8,8,128]{4,3,2,1,0:T(8,128)}, u32[]{:S(2)}) copy-start(f32[4,8,8,8,128]{4,3,2,1,0:T(8,128)} %param.19) | copy-start | bytes 3145732
  43.9 4.3 %copy-start.11 = (f32[128,128,1,1,1]{1,0,4,3,2:T(8,128)S(1)}, f32[128,128,1,1,1]{1,0,4,3,2:T(8,128)}, u32[]{:S(2)}) copy-start(f32[128,128,1,1,1]{1,0,4,3,2:T(8,128)} %constant.38) | copy-start | bytes 196612
  45.4 3.8 %copy-start.4 = (f32[4,8,8,8,128]{4,3,2,1,0:T(8,128)}, f32[4,8,8,8,128]{4,3,2,1,0:T(8,128)S(1)}, u32[]{:S(2)}) copy-start(f32[4,8,8,8,128]{4,3,2,1,0:T(8,128)S(1)} %get-tuple-element.5) | copy-start | bytes 3145732
  49.2 79.2 %copy-start.10 = (f32[128,128,1,1,1]{1,0,4,3,2:T(8,128)S(1)}, f32[128,128,1,1,1]{1,0,4,3,2:T(8,128)}, u32[]{:S(2)}) copy-start(f32[128,128,1,1,1]{1,0,4,3,2:T(8,128)} %constant.39) | copy-start | bytes 196612
  131.6 6.5 %collective-permute-start.4 = (f32[1,57,128]{2,0,1:T(1,128)S(1)}, f32[1,57,128]{2,0,1:T(1,128)S(1)}, u32[]{:S(2)}, u32[]{:S(2)}) collective-permute-start(f32[1,57,128]{2,0,1:T(1,128)S(1)} %pad_maximum_fusion.9), channel_id=1, source_target_pairs={{0,64},{64,128},{128,192},{1,65},{65,129},{129,193},{2,66},{66,130... | collective-permute-start | bytes 87560 | tf_op jit(solution)/shard_map/ppermute | solution.py:29
  138.1 7.4 %collective-permute-start.5 = (f32[1,57,128]{2,0,1:T(1,128)S(1)}, f32[1,57,128]{2,0,1:T(1,128)S(1)}, u32[]{:S(2)}, u32[]{:S(2)}) collective-permute-start(f32[1,57,128]{2,0,1:T(1,128)S(1)} %get-tuple-element.3), channel_id=1, source_target_pairs={{64,0},{128,64},{192,128},{65,1},{129,65},{193,129},{66,2},{130,66... | collective-permute-start | bytes 87560 | tf_op jit(solution)/shard_map/ppermute | solution.py:31
  145.7 8.7 %collective-permute-start.6 = (f32[29,1,128]{2,0,1:T(8,128)S(1)}, f32[29,1,128]{2,0,1:T(8,128)S(1)}, u32[]{:S(2)}, u32[]{:S(2)}) collective-permute-start(f32[29,1,128]{2,0,1:T(8,128)S(1)} %get-tuple-element.18), channel_id=1, source_target_pairs={{0,1},{1,2},{2,3},{3,4},{4,5},{5,6},{6,7},{7,8},{8,9},{9,10},{10,1... | collective-permute-start | bytes 44552 | tf_op jit(solution)/shard_map/ppermute | solution.py:29
  152.4 7.2 %collective-permute-start.7 = (f32[29,1,128]{2,0,1:T(8,128)S(1)}, f32[29,1,128]{2,0,1:T(8,128)S(1)}, u32[]{:S(2)}, u32[]{:S(2)}) collective-permute-start(f32[29,1,128]{2,0,1:T(8,128)S(1)} %get-tuple-element.19), channel_id=1, source_target_pairs={{1,0},{2,1},{3,2},{4,3},{5,4},{6,5},{7,6},{8,7},{9,8},{10,9},{11,1... | collective-permute-start | bytes 44552 | tf_op jit(solution)/shard_map/ppermute | solution.py:31
where the time goes:
time: 162 us
  blocking collectives  74.8 us (46%)
  starting transfers between devices  31.2 us (19%)
  matrix products  23.6 us (15%)
  waiting for transfers between devices  22.8 us (14%)
  other arithmetic  4.33 us (3%)
  local copies, waits for them, and re-layouts  3.74 us (2%)
    psum x1, blocking collectives, body(): inner_vector = lax.psum(partial_inner, ('grp', 'dev'))  74.8 us
    ppermute x4, starting transfers between devices, extended(): lax.ppermute(tail, axis, [(i, (i + 1) % count) for i in range(ends)])  23.5 us
    ppermute x4, waiting for transfers between devices, extended(): lax.ppermute(head, axis, [((i + 1) % count, i) for i in range(ends)])  20.9 us
    dot_general x4, matrix products, along_first(): jnp.einsum('ai,xiyjz->xayjz', matrix, field, precision=HIGHEST_PRECISION)  8.94 us
    ppermute x4, starting transfers between devices, extended(): lax.ppermute(head, axis, [((i + 1) % count, i) for i in range(ends)])  7.68 us
    dot_general x4, matrix products, along_second(): jnp.einsum('bj,xiyjz->xiybz', matrix, field, precision=HIGHEST_PRECISION)  6.77 us
    dot_general x6, matrix products, along_third(): jnp.einsum('xiyjz,zw->xiyjw', field, table, precision=HIGHEST_PRECISION)  6.37 us
  transfers between devices with their start and end apart: 8, of which 6 were waited for; matrix products, arithmetic and copies ran while one was open for 0% of the time, Pallas kernels for 0%

commit v1 on v0

v1 whole, which is shorter than its diff:
```python
import functools
import math

import jax
import jax.numpy as jnp
import ml_dtypes
import numpy as np
from jax import lax
from jax.experimental import pallas as pl
from jax.experimental.pallas import tpu as pltpu
from jax.sharding import PartitionSpec as P

GLL_POINTS = [
    -1.0,
    -0.871740148509607,
    -0.591700181433142,
    -0.209299217902479,
    0.209299217902479,
    0.591700181433142,
    0.871740148509607,
    1.0,
]


def legendre_value(point, highest):
    previous = 1.0
    current = point
    for degree in range(1, highest):
        previous, current = (
            current,
            ((2 * degree + 1) * point * current - degree * previous) / (degree + 1),
        )
    return current


def identity_list(dimension):
    return [
        [1.0 if row_index == col_index else 0.0 for col_index in range(dimension)]
        for row_index in range(dimension)
    ]


def transpose_list(matrix):
    return [
        [matrix[row_index][col_index] for row_index in range(len(matrix))]
        for col_index in range(len(matrix[0]))
    ]


def matrix_product(left, right):
    inner_size = len(right)
    return [
        [
            sum((left[row_index][inner] * right[inner][col_index] for inner in range(inner_size)))
            for col_index in range(len(right[0]))
        ]
        for row_index in range(len(left))
    ]


def jacobi_eigen(matrix):
    current = [list(line) for line in matrix]
    dimension = len(matrix)
    rotations = identity_list(dimension)
    for repeat in range(12):
        for row_index in range(dimension - 1):
            for col_index in range(row_index + 1, dimension):
                angle = 0.5 * math.atan2(
                    2.0 * current[row_index][col_index],
                    current[row_index][row_index] - current[col_index][col_index],
                )
                cosine = math.cos(angle)
                sine_value = math.sin(angle)
                rotation = identity_list(dimension)
                rotation[row_index][row_index] = cosine
                rotation[col_index][col_index] = cosine
                rotation[row_index][col_index] = -sine_value
                rotation[col_index][row_index] = sine_value
                current = matrix_product(
                    matrix_product(transpose_list(rotation), current), rotation
                )
                rotations = matrix_product(rotations, rotation)
    ordering = sorted(range(dimension), key=lambda position: current[position][position])
    return [
        [rotations[row_index][position] for position in ordering] for row_index in range(dimension)
    ]


def element_tables():
    total_points = len(GLL_POINTS)
    weights_bary = []
    for row_index in range(total_points):
        product_value = 1.0
        for col_index in range(total_points):
            if col_index != row_index:
                product_value = product_value * (GLL_POINTS[row_index] - GLL_POINTS[col_index])
        weights_bary.append(1.0 / product_value)
    derivative = [[0.0] * total_points for row_index in range(total_points)]
    for row_index in range(total_points):
        for col_index in range(total_points):
            if col_index != row_index:
                derivative[row_index][col_index] = (
                    weights_bary[col_index]
                    / weights_bary[row_index]
                    / (GLL_POINTS[row_index] - GLL_POINTS[col_index])
                )
        derivative[row_index][row_index] = -sum(derivative[row_index])
    quadrature = [
        2.0 / ((total_points - 1) * total_points * legendre_value(point, total_points - 1) ** 2)
        for point in GLL_POINTS
    ]
    stiffness = [
        [
            sum(
                (
                    derivative[inner][row_index] * quadrature[inner] * derivative[inner][col_index]
                    for inner in range(total_points)
                )
            )
            + (quadrature[row_index] if row_index == col_index else 0.0)
            for col_index in range(total_points)
        ]
        for row_index in range(total_points)
    ]
    return (derivative, jacobi_eigen(stiffness))


def block_diagonal(blocks, matrix):
    node_count = len(matrix)
    total = blocks * node_count
    return [
        [
            (
                matrix[row_index % node_count][col_index % node_count]
                if row_index // node_count == col_index // node_count
                else 0.0
            )
            for col_index in range(total)
        ]
        for row_index in range(total)
    ]


def assembly_table(blocks, node_count):
    total = blocks * node_count
    shared_index = [
        position // node_count * (node_count - 1) + position % node_count
        for position in range(total)
    ]
    return [
        [
            1.0 if shared_index[row_index] == shared_index[col_index] else 0.0
            for col_index in range(total)
        ]
        for row_index in range(total)
    ]

MESH_IDS = pl.DeviceIdType.MESH
TILE = 128
PACK = 16


def split_halves(values):
    high = values.astype(jnp.bfloat16)
    return high, (values - high.astype(jnp.float32)).astype(jnp.bfloat16)


def lane_operator(table, field):
    high, low = split_halves(field)
    stacked = jnp.concatenate([table, table], axis=0)
    product = jnp.dot(
        jnp.concatenate([high, low], axis=1), stacked, preferred_element_type=jnp.float32
    )
    return product[:, :TILE] + product[:, TILE:]


def row_operator(table, field):
    high, low = split_halves(field)
    stacked = jnp.concatenate([table, table], axis=1)
    results = []
    for start in range(0, field.shape[0], 2 * TILE):
        first, second = slice(start, start + TILE), slice(start + TILE, start + 2 * TILE)
        operand = jnp.concatenate(
            [
                jnp.concatenate([high[first], low[first]], axis=0),
                jnp.concatenate([high[second], low[second]], axis=0),
            ],
            axis=1,
        )
        product = jnp.dot(stacked, operand, preferred_element_type=jnp.float32)
        summed = product[:TILE] + product[TILE:]
        results += [summed[:, :TILE], summed[:, TILE:]]
    return jnp.concatenate(results, axis=0)


def weighted(coefficients, terms):
    total = terms[0] * coefficients[0]
    for coefficient, term in zip(coefficients[1:], terms[1:]):
        total = total + term * coefficient
    return total


def mirrored(layers):
    count = len(layers)
    half = count // 2
    sums = [layers[k] + layers[count - 1 - k] for k in range(half)]
    gaps = [layers[k] - layers[count - 1 - k] for k in range(half)]
    return sums, gaps


def odd_operator(matrix, layers):
    count = len(layers)
    half = count // 2
    sums, gaps = mirrored(layers)
    lower, upper = [], []
    for row in range(half):
        line = matrix[row]
        even = weighted([0.5 * (line[k] + line[count - 1 - k]) for k in range(half)], sums)
        odd = weighted([0.5 * (line[k] - line[count - 1 - k]) for k in range(half)], gaps)
        lower.append(odd + even)
        upper.append(odd - even)
    return lower + upper[::-1]


def to_modes(vectors, layers):
    count = len(layers)
    half = count // 2
    sums, gaps = mirrored(layers)
    return [
        weighted([vectors[k][mode] for k in range(half)], gaps if mode % 2 else sums)
        for mode in range(count)
    ]


def from_modes(vectors, modes):
    count = len(modes)
    half = count // 2
    lower, upper = [], []
    for row in range(half):
        even = weighted(vectors[row][0::2], modes[0::2])
        odd = weighted(vectors[row][1::2], modes[1::2])
        lower.append(even + odd)
        upper.append(even - odd)
    return lower + upper[::-1]


def half_pair(matrix):
    table = np.asarray(matrix, np.float64).astype(np.float32)
    high = table.astype(ml_dtypes.bfloat16)
    low = (table - high.astype(np.float32)).astype(ml_dtypes.bfloat16)
    return high, low


def lane_table(matrix):
    return np.concatenate(half_pair(matrix), axis=1)


def row_table(matrix):
    return np.concatenate(half_pair(matrix), axis=0)


def operator_tables(nodes, lanes):
    derivative, vectors = element_tables()
    blocks = lanes // nodes
    backward_z = block_diagonal(blocks, derivative)
    vectors_z = block_diagonal(blocks, vectors)
    joined = assembly_table(blocks, nodes)
    physical_joined = (np.asarray(transpose_list(vectors_z)) @ np.asarray(joined)).tolist()
    lane_tables = np.stack(
        [
            lane_table(transpose_list(backward_z)),
            lane_table(backward_z),
            lane_table(vectors_z),
            lane_table(physical_joined),
        ]
    )
    row_tables = np.stack(
        [
            row_table(backward_z),
            row_table(transpose_list(backward_z)),
            row_table(transpose_list(vectors_z)),
            row_table(vectors_z),
        ]
    )
    return derivative, vectors, lane_tables, row_tables


class Layout:
    def __init__(self, elements_x, nodes, elements_y, lanes, groups, devices, coarse):
        self.ex, self.n, self.ey, self.lanes = elements_x, nodes, elements_y, lanes
        self.groups, self.devices = groups, devices
        self.slab = elements_y * nodes
        self.chunk = nodes * self.slab
        self.rows = elements_x * self.chunk
        self.lines = elements_x * nodes
        self.columns = elements_x * elements_y
        self.pack = math.gcd(PACK, devices)
        self.far = groups * (devices // self.pack)
        self.coarse = coarse
        self.coarse_lines = coarse // lanes
        self.share = self.coarse_lines // self.pack


def step_kernel(
    lay, derivative, vectors,
    adjoint, right_side, velocity, conductivity, mass_term, fdm_inverse, factor, lane_t, row_t,
    residual, correction,
    v_adj, v_rs, v_vel, v_con, v_mass, v_fdm, v_fac, v_lane, v_row,
    local, side_send, side_recv, row_send, row_recv, edge_recv, halo_lines,
    column_sum, inner_part, near_src, near_in, far_in, full_in,
    own_coarse, ring_x, ring_y, ring_d, grid_rows, coarse_tile,
    load_sem, face_send, face_recv, ring_send, ring_recv, sum_send, sum_recv,
):
    ex, n, ey, lanes = lay.ex, lay.n, lay.ey, lay.lanes
    slab, chunk, lines, columns = lay.slab, lay.chunk, lay.lines, lay.columns
    group = lax.axis_index("grp")
    device = lax.axis_index("dev")
    near_id = lax.rem(device, lay.pack)
    block_id = device // lay.pack
    far_blocks = lay.devices // lay.pack
    far_id = group * far_blocks + block_id

    def near_device(index):
        return (group, block_id * lay.pack + index)

    def far_device(index):
        return (index // far_blocks, lax.rem(index, far_blocks) * lay.pack + near_id)

    def neighbour(step_g, step_d):
        return (
            lax.rem(group + step_g + lay.groups, lay.groups),
            lax.rem(device + step_d + lay.devices, lay.devices),
        )

    steps = [(g, d) for g in (-1, 0, 1) for d in (-1, 0, 1) if (g, d) != (0, 0)]

    barrier = pltpu.get_barrier_semaphore()
    for step in steps:
        pl.semaphore_signal(barrier, inc=1, device_id=neighbour(*step), device_id_type=MESH_IDS)
    for offset in range(1, lay.pack):
        target = near_device(lax.rem(near_id + offset, lay.pack))
        pl.semaphore_signal(barrier, inc=1, device_id=target, device_id_type=MESH_IDS)
    for offset in range(1, lay.far):
        target = far_device(lax.rem(far_id + offset, lay.far))
        pl.semaphore_signal(barrier, inc=1, device_id=target, device_id_type=MESH_IDS)

    def chunk_rows(x):
        return pl.ds(pl.multiple_of(x * chunk, chunk), chunk)

    def chunk_loads(x):
        rows = chunk_rows(x)
        return [
            pltpu.make_async_copy(adjoint.at[rows], v_adj.at[rows], load_sem.at[0, x]),
            pltpu.make_async_copy(conductivity.at[rows], v_con.at[rows], load_sem.at[1, x]),
            pltpu.make_async_copy(velocity.at[:, rows], v_vel.at[:, rows], load_sem.at[2, x]),
            pltpu.make_async_copy(mass_term.at[rows], v_mass.at[rows], load_sem.at[3, x]),
        ]

    table_loads = [
        pltpu.make_async_copy(lane_t, v_lane, load_sem.at[4, 0]),
        pltpu.make_async_copy(row_t, v_row, load_sem.at[4, 1]),
    ]
    late_loads = [
        pltpu.make_async_copy(right_side, v_rs, load_sem.at[4, 2]),
        pltpu.make_async_copy(factor, v_fac, load_sem.at[4, 3]),
        pltpu.make_async_copy(fdm_inverse, v_fdm, load_sem.at[5, 0]),
    ]
    for copy in table_loads:
        copy.start()
    for x in range(ex):
        for copy in chunk_loads(x):
            copy.start()
    for copy in late_loads:
        copy.start()
    for copy in table_loads:
        copy.wait()

    lane_index = lax.broadcasted_iota(jnp.int32, (1, lanes), 1)
    lane_node = lax.rem(lane_index, n)
    is_upper = lane_node == n - 1
    shared = jnp.where(
        (is_upper & (lane_index != lanes - 1)) | ((lane_node == 0) & (lane_index != 0)), 1.0, 0.0
    ).astype(jnp.float32)
    line_index = lax.broadcasted_iota(jnp.int32, (n, lanes), 0)
    first_line = line_index == 0
    last_line = line_index == n - 1

    def layers_of(field):
        return [field[k * slab : (k + 1) * slab] for k in range(n)]

    def local_chunk(x, carry):
        for copy in chunk_loads(x):
            copy.wait()
        rows = chunk_rows(x)
        field = v_adj[rows]
        diffusion = v_con[rows]
        third = diffusion * lane_operator(v_lane[0], field) + v_vel[2, rows] * field
        total = lane_operator(v_lane[1], third)
        second = diffusion * row_operator(v_row[0], field) + v_vel[1, rows] * field
        total = total + row_operator(v_row[1], second)
        gradient = jnp.concatenate(odd_operator(derivative, layers_of(field)), axis=0)
        first = diffusion * gradient + v_vel[0, rows] * field
        total = total + jnp.concatenate(
            odd_operator(transpose_list(derivative), layers_of(first)), axis=0
        )
        total = total + v_mass[rows] * field
        crossed = jnp.where(
            is_upper, pltpu.roll(total, lanes - 1, axis=1), pltpu.roll(total, 1, axis=1)
        )
        local[rows] = total + shared * crossed
        return carry

    lax.fori_loop(0, ex, local_chunk, 0)

    low_g = jnp.where(group > 0, 1.0, 0.0).astype(jnp.float32)
    high_g = jnp.where(group < lay.groups - 1, 1.0, 0.0).astype(jnp.float32)
    low_d = jnp.where(device > 0, 1.0, 0.0).astype(jnp.float32)
    high_d = jnp.where(device < lay.devices - 1, 1.0, 0.0).astype(jnp.float32)
    gates_g, gates_d = (low_g, high_g), (low_d, high_d)

    def face_copies(phase):
        copies = []
        for index, (g, d) in enumerate(steps):
            if d == 0:
                source, target = side_send.at[phase, (g + 1) // 2], side_recv.at[phase, (1 - g) // 2]
            elif g == 0:
                source, target = row_send.at[phase, (d + 1) // 2], row_recv.at[phase, (1 - d) // 2]
            else:
                x = 0 if g < 0 else ex - 1
                source = row_send.at[phase, (d + 1) // 2, x]
                target = edge_recv.at[phase, (1 - g) // 2, (1 - d) // 2]
            copies.append(
                pltpu.make_async_remote_copy(
                    src_ref=source,
                    dst_ref=target,
                    send_sem=face_send.at[phase, index],
                    recv_sem=face_recv.at[phase, index],
                    device_id=neighbour(g, d),
                    device_id_type=MESH_IDS,
                )
            )
        return copies

    def send_faces(field, phase):
        side_send[phase, 0] = field[pl.ds(0, slab)]
        side_send[phase, 1] = field[pl.ds(lay.rows - slab, slab)]
        for x in range(ex - 1):
            upper, lower = pl.ds((x + 1) * chunk - slab, slab), pl.ds((x + 1) * chunk, slab)
            both = field[upper] + field[lower]
            field[upper] = both
            field[lower] = both
        for x in range(ex):
            row_send[phase, 0, x] = field[pl.ds(x * chunk, n, stride=slab)]
            row_send[phase, 1, x] = field[pl.ds(x * chunk + slab - 1, n, stride=slab)]
        copies = face_copies(phase)
        for copy in copies:
            copy.start()
        return copies

    def join_faces(field, phase, copies):
        for copy in copies:
            copy.wait_recv()
        head, tail = pl.ds(0, slab), pl.ds(lay.rows - slab, slab)
        field[head] = field[head] + low_g * side_recv[phase, 0]
        field[tail] = field[tail] + high_g * side_recv[phase, 1]
        for d in range(2):
            low_edge = edge_recv[phase, 0, d, pl.ds(n - 1, n, stride=0)]
            high_edge = edge_recv[phase, 1, d, pl.ds(0, n, stride=0)]
            first = row_recv[phase, d, 0] + jnp.where(first_line, low_g * low_edge, 0.0)
            row_recv[phase, d, 0] = first
            last = row_recv[phase, d, ex - 1] + jnp.where(last_line, high_g * high_edge, 0.0)
            row_recv[phase, d, ex - 1] = last
            spot = 0 if d == 0 else n - 1
            for x in range(ex):
                halo_lines[pl.ds(x * slab + spot, n, stride=n)] = gates_d[d] * row_recv[phase, d, x]
        starts = pl.ds(0, lines * ey, stride=n)
        ends = pl.ds(n - 1, lines * ey, stride=n)
        lower = field[starts].reshape(lines, ey, lanes)
        upper = field[ends].reshape(lines, ey, lanes)
        outside = halo_lines[...].reshape(lines, ey, lanes)
        from_below = jnp.where(first_line, outside, pltpu.roll(upper, 1, axis=1))
        from_above = jnp.where(last_line, outside, pltpu.roll(lower, ey - 1, axis=1))
        field[starts] = (lower + from_below).reshape(lines * ey, lanes)
        field[ends] = (upper + from_above).reshape(lines * ey, lanes)

    pl.semaphore_wait(barrier, len(steps) + lay.pack - 1 + lay.far - 1)
    first_copies = send_faces(local, 0)
    for copy in late_loads:
        copy.wait()
    join_faces(local, 0, first_copies)

    for x in range(ex):
        rows = pl.ds(x * chunk, chunk)
        value = v_rs[rows] - local[rows]
        residual[rows] = value
        layers = layers_of(value)
        total = layers[0]
        for layer in layers[1:]:
            total = total + layer
        column_sum[pl.ds(x * slab, slab)] = total
    summed = column_sum[pl.ds(0, columns, stride=n)]
    for j in range(1, n):
        summed = summed + column_sum[pl.ds(j, columns, stride=n)]
    means = jnp.sum(summed, axis=1, keepdims=True) * (1.0 / float(n * n * lanes))
    means = jnp.broadcast_to(means, (columns, lanes))

    def inner_block(block, carry):
        for k in range(8):
            line = block * 8 + k
            piece = v_fac[:, pl.ds(pl.multiple_of(line * lanes, lanes), lanes)] * means
            total = piece[0:8]
            for start in range(8, columns, 8):
                total = total + piece[start : start + 8]
            inner_part[pl.ds(pl.multiple_of(line * 8, 8), 8)] = total
        return carry

    lax.fori_loop(0, lay.coarse_lines // 8, inner_block, 0)
    for index in range(lay.pack):
        base = index * lay.share * 8
        total = inner_part[pl.ds(base, lay.share, stride=8)]
        for k in range(1, 8):
            total = total + inner_part[pl.ds(base + k, lay.share, stride=8)]
        near_src[index] = total

    def exchange(stage, count, own, device_of, source_of, buffer):
        def send(offset, carry):
            index = lax.rem(own + offset, count)
            pltpu.make_async_remote_copy(
                src_ref=source_of(index),
                dst_ref=buffer.at[own],
                send_sem=sum_send.at[stage],
                recv_sem=sum_recv.at[stage],
                device_id=device_of(index),
                device_id_type=MESH_IDS,
            ).start()
            return carry

        for offset in range(1, count):
            send(offset, 0)

    def await_exchange(stage, count, buffer, sem):
        part = buffer.at[pl.ds(0, count - 1)]
        pltpu.make_async_copy(part, part, sem.at[stage]).wait()

    exchange(0, lay.pack, near_id, near_device, lambda index: near_src.at[index], near_in)
    near_in[near_id] = near_src[near_id]

    def solve_chunk(x, carry):
        rows = chunk_rows(x)
        field = jnp.concatenate(to_modes(vectors, layers_of(residual[rows])), axis=0)
        field = row_operator(v_row[2], field)
        field = lane_operator(v_lane[2], field) * v_fdm[rows]
        field = lane_operator(v_lane[3], field)
        field = row_operator(v_row[3], field)
        correction[rows] = jnp.concatenate(from_modes(vectors, layers_of(field)), axis=0)
        return carry

    third = ex // 2
    lax.fori_loop(0, third, solve_chunk, 0)

    await_exchange(0, lay.pack, near_in, sum_recv)
    far_in[far_id] = jnp.sum(near_in[...], axis=0)
    exchange(1, lay.far, far_id, far_device, lambda index: far_in.at[far_id], far_in)

    lax.fori_loop(third, ex, solve_chunk, 0)
    second_copies = send_faces(correction, 1)

    await_exchange(1, lay.far, far_in, sum_recv)
    full_in[near_id] = jnp.sum(far_in[...], axis=0)
    exchange(2, lay.pack, near_id, near_device, lambda index: full_in.at[near_id], full_in)

    join_faces(correction, 1, second_copies)

    await_exchange(2, lay.pack, full_in, sum_recv)

    def value_block(index, total):
        for k in range(lay.share):
            line = index * lay.share + k
            value = jnp.broadcast_to(full_in[index, pl.ds(k, 1)], (columns, lanes))
            total = total + v_fac[:, pl.ds(pl.multiple_of(line * lanes, lanes), lanes)] * value
        return total

    totals = lax.fori_loop(0, lay.pack, value_block, jnp.zeros((columns, lanes), jnp.float32))
    values = jnp.broadcast_to(jnp.sum(totals, axis=1, keepdims=True), (columns, lanes))
    own_coarse[...] = values.reshape(ex, ey, lanes)

    ring_copies = []
    for index, (g, d) in enumerate(steps):
        x = 0 if g < 0 else ex - 1
        if d == 0:
            source, target = own_coarse.at[x], ring_x.at[(1 - g) // 2]
        elif g == 0:
            source, target = own_coarse, ring_y.at[(1 - d) // 2]
        else:
            source, target = own_coarse.at[x], ring_d.at[(1 - g) // 2, (1 - d) // 2]
        copy = pltpu.make_async_remote_copy(
            src_ref=source,
            dst_ref=target,
            send_sem=ring_send.at[index],
            recv_sem=ring_recv.at[index],
            device_id=neighbour(g, d),
            device_id_type=MESH_IDS,
        )
        copy.start()
        ring_copies.append(copy)
    for copy in ring_copies:
        copy.wait_recv()

    def padded(inside, below, above):
        return [low_g * below] + inside + [high_g * above]

    center = padded([own_coarse[x] for x in range(ex)], ring_x[0], ring_x[1])
    left = padded([ring_y[0, x] for x in range(ex)], ring_d[0, 0], ring_d[1, 0])
    right = padded([ring_y[1, x] for x in range(ex)], ring_d[0, 1], ring_d[1, 1])
    twice = 1.0 + shared
    for x in range(ex):
        rows = x * chunk
        for part in range(3):
            def joined(values):
                value = values[x + 1]
                if part == 0:
                    value = value + values[x]
                elif part == 2:
                    value = value + values[x + 2]
                return value * twice

            inside = joined(center)
            before = low_d * pltpu.roll(joined(left), 1, axis=0)
            after = high_d * pltpu.roll(joined(right), ey - 1, axis=0)
            below = jnp.where(first_line, before, pltpu.roll(inside, 1, axis=0))
            above = jnp.where(last_line, after, pltpu.roll(inside, ey - 1, axis=0))
            for j in range(n):
                value = inside
                if j == 0:
                    value = inside + below
                elif j == n - 1:
                    value = inside + above
                coarse_tile[part, pl.ds(j, ey, stride=n)] = value
            layers = {0: [0], 1: list(range(1, n - 1)), 2: [n - 1]}[part]
            tile = coarse_tile[part]
            for layer in layers:
                spot = pl.ds(rows + layer * slab, slab)
                correction[spot] = correction[spot] + tile

    for copy in first_copies + second_copies + ring_copies:
        copy.wait_send()
    await_exchange(0, lay.pack, near_in, sum_send)
    await_exchange(1, lay.far, far_in, sum_send)
    await_exchange(2, lay.pack, full_in, sum_send)


def solution(mesh):
    groups, devices = mesh.shape["grp"], mesh.shape["dev"]

    def body(adjoint, right_side, velocity, conductivity, mass_term, fdm_inverse, coarse_factor):
        ex, n, ey, _, lanes = adjoint.shape
        lay = Layout(ex, n, ey, lanes, groups, devices, coarse_factor.shape[1])
        derivative, vectors, lane_tables, row_tables = operator_tables(n, lanes)
        flat = (lay.rows, lanes)
        f32, bf16 = jnp.float32, jnp.bfloat16
        anywhere = pl.BlockSpec(memory_space=pltpu.HBM)
        vmem = pl.BlockSpec(memory_space=pltpu.VMEM)
        scratch = [
            pltpu.VMEM(flat, f32),
            pltpu.VMEM(flat, f32),
            pltpu.VMEM((3,) + flat, f32),
            pltpu.VMEM(flat, f32),
            pltpu.VMEM(flat, f32),
            pltpu.VMEM(flat, f32),
            pltpu.VMEM(coarse_factor.shape, f32),
            pltpu.VMEM(lane_tables.shape, bf16),
            pltpu.VMEM(row_tables.shape, bf16),
            pltpu.VMEM(flat, f32),
            pltpu.VMEM((2, 2, lay.slab, lanes), f32),
            pltpu.VMEM((2, 2, lay.slab, lanes), f32),
            pltpu.VMEM((2, 2, ex, n, lanes), f32),
            pltpu.VMEM((2, 2, ex, n, lanes), f32),
            pltpu.VMEM((2, 2, 2, n, lanes), f32),
            pltpu.VMEM((lay.lines * ey, lanes), f32),
            pltpu.VMEM((ex * lay.slab, lanes), f32),
            pltpu.VMEM((lay.coarse_lines * 8, lanes), f32),
            pltpu.VMEM((lay.pack, lay.share, lanes), f32),
            pltpu.VMEM((lay.pack, lay.share, lanes), f32),
            pltpu.VMEM((lay.far, lay.share, lanes), f32),
            pltpu.VMEM((lay.pack, lay.share, lanes), f32),
            pltpu.VMEM((ex, ey, lanes), f32),
            pltpu.VMEM((2, ey, lanes), f32),
            pltpu.VMEM((2, ex, ey, lanes), f32),
            pltpu.VMEM((2, 2, ey, lanes), f32),
            pltpu.VMEM((8, lanes), f32),
            pltpu.VMEM((3, lay.slab, lanes), f32),
            pltpu.SemaphoreType.DMA((6, 4)),
            pltpu.SemaphoreType.DMA((2, 8)),
            pltpu.SemaphoreType.DMA((2, 8)),
            pltpu.SemaphoreType.DMA((8,)),
            pltpu.SemaphoreType.DMA((8,)),
            pltpu.SemaphoreType.DMA((3,)),
            pltpu.SemaphoreType.DMA((3,)),
        ]
        residual, correction = pl.pallas_call(
            functools.partial(step_kernel, lay, derivative, vectors),
            out_shape=[jax.ShapeDtypeStruct(flat, f32)] * 2,
            in_specs=[anywhere] * 9,
            out_specs=[vmem, vmem],
            scratch_shapes=scratch,
            compiler_params=pltpu.CompilerParams(
                collective_id=0, has_side_effects=True, vmem_limit_bytes=40 * 1024 * 1024
            ),
            name="adjoint_step",
        )(
            *[
                pltpu.with_memory_space_constraint(array, pltpu.HBM)
                for array in (
                    adjoint.reshape(flat),
                    right_side.reshape(flat),
                    velocity.reshape((3,) + flat),
                    conductivity.reshape(flat),
                    mass_term.reshape(flat),
                    fdm_inverse.reshape(flat),
                    coarse_factor,
                    jnp.asarray(lane_tables),
                    jnp.asarray(row_tables),
                )
            ]
        )
        return residual.reshape(adjoint.shape), correction.reshape(adjoint.shape)

    field = P("grp", None, "dev", None, None)
    in_specs = (
        field,
        field,
        P(None, "grp", None, "dev", None, None),
        field,
        field,
        field,
        P(("grp", "dev"), None),
    )
    return jax.shard_map(
        body, mesh=mesh, in_specs=in_specs, out_specs=(field, field), check_vma=False
    )
```

time: 162 us -> 39.8 us (0.25)
  the two profiles are of different devices: /device:TPU:71 before, /device:TPU:1 now
where the time goes in v1:
time: 39.8 us; the launch traced here: 39.7 us
  Pallas kernels  37.1 us (93%)
  local copies, waits for them, and re-layouts  1.94 us (5%)
  between operations  0.64 us (2%)
    pallas_call x1, Pallas kernels, body(): pl.pallas_call(functools.partial(step_kernel, lay, derivative, vectors),...  37.1 us
    unnamed x2, local copies, waits for them, and re-layouts  1.94 us

profile of v1, /device:TPU:1, one launch (start us, length us, event | category | flops | bytes accessed | tf_op | source)
XLA Modules:
  0.0 39.7 jit_solution(6761361576301202461)
XLA Ops:
  0.6 37.1 %adjoint_step.1 = (f32[2048,128]{1,0:T(8,128)S(1)}, f32[2048,128]{1,0:T(8,128)S(1)}) custom-call(f32[2048,128]{1,0:T(8,128)} %bitcast.11, f32[2048,128]{1,0:T(8,128)} %bitcast.12, f32[3,2048,128]{2,1,0:T(8,128)} %bitcast.10, f32[2048,128]{1,0:T(8,128)} %bitcast.13, f32[2048,128]{1,0:T(8,128)} %bitcast.14, f32[2048,128]{1,0:T(8,128)} %bitcast.15, ...), custom_call_target="tpu_custom_call" | custom-call | tf_op jit(solution)/shard_map/adjoint_step/pallas_call | solution.py:700
  37.8 1.0 %copy.13 = f32[4,8,8,8,128]{4,3,2,1,0:T(8,128)} copy(f32[4,8,8,8,128]{4,3,2,1,0:T(8,128)S(1)} %bitcast.9) | data formatting | bytes 2097152
  38.7 1.0 %copy.14 = f32[4,8,8,8,128]{4,3,2,1,0:T(8,128)} copy(f32[4,8,8,8,128]{4,3,2,1,0:T(8,128)S(1)} %bitcast.8) | data formatting | bytes 2097152

commit v2 on v1

--- a/solution.py
+++ b/solution.py
@@ -304,12 +304,12 @@
 def step_kernel(
     lay, derivative, vectors,
     adjoint, right_side, velocity, conductivity, mass_term, fdm_inverse, factor, lane_t, row_t,
-    residual, correction,
+    residual, correction, grid,
     v_adj, v_rs, v_vel, v_con, v_mass, v_fdm, v_fac, v_lane, v_row,
     local, side_send, side_recv, row_send, row_recv, edge_recv, halo_lines,
     column_sum, inner_part, near_src, near_in, far_in, full_in,
-    own_coarse, ring_x, ring_y, ring_d, grid_rows, coarse_tile,
-    load_sem, face_send, face_recv, ring_send, ring_recv, sum_send, sum_recv,
+    sum_tile, note_send, note_recv, rim_send, rim_recv, ring_out, ring_in,
+    load_sem, face_send, face_recv, note_sent, note_got, rim_sem, ring_sem, sum_send, sum_recv,
 ):
     ex, n, ey, lanes = lay.ex, lay.n, lay.ey, lay.lanes
     slab, chunk, lines, columns = lay.slab, lay.chunk, lay.lines, lay.columns
@@ -334,6 +334,33 @@
 
     steps = [(g, d) for g in (-1, 0, 1) for d in (-1, 0, 1) if (g, d) != (0, 0)]
 
+    def chunk_rows(x):
+        return pl.ds(pl.multiple_of(x * chunk, chunk), chunk)
+
+    def chunk_loads(x):
+        rows = chunk_rows(x)
+        return [
+            pltpu.make_async_copy(adjoint.at[rows], v_adj.at[rows], load_sem.at[0, x]),
+            pltpu.make_async_copy(conductivity.at[rows], v_con.at[rows], load_sem.at[1, x]),
+            pltpu.make_async_copy(velocity.at[:, rows], v_vel.at[:, rows], load_sem.at[2, x]),
+            pltpu.make_async_copy(mass_term.at[rows], v_mass.at[rows], load_sem.at[3, x]),
+        ]
+
+    def table_loads(part):
+        half = pl.ds(2 * part, 2)
+        return [
+            pltpu.make_async_copy(lane_t.at[half], v_lane.at[half], load_sem.at[4 + part, 0]),
+            pltpu.make_async_copy(row_t.at[half], v_row.at[half], load_sem.at[4 + part, 1]),
+        ]
+
+    late_loads = [
+        pltpu.make_async_copy(right_side, v_rs, load_sem.at[4, 2]),
+        pltpu.make_async_copy(factor, v_fac, load_sem.at[4, 3]),
+        pltpu.make_async_copy(fdm_inverse, v_fdm, load_sem.at[5, 2]),
+    ] + table_loads(1)
+    for copy in chunk_loads(0) + table_loads(0):
+        copy.start()
+
     barrier = pltpu.get_barrier_semaphore()
     for step in steps:
         pl.semaphore_signal(barrier, inc=1, device_id=neighbour(*step), device_id_type=MESH_IDS)
@@ -344,36 +371,6 @@
         target = far_device(lax.rem(far_id + offset, lay.far))
         pl.semaphore_signal(barrier, inc=1, device_id=target, device_id_type=MESH_IDS)
 
-    def chunk_rows(x):
-        return pl.ds(pl.multiple_of(x * chunk, chunk), chunk)
-
-    def chunk_loads(x):
-        rows = chunk_rows(x)
-        return [
-            pltpu.make_async_copy(adjoint.at[rows], v_adj.at[rows], load_sem.at[0, x]),
-            pltpu.make_async_copy(conductivity.at[rows], v_con.at[rows], load_sem.at[1, x]),
-            pltpu.make_async_copy(velocity.at[:, rows], v_vel.at[:, rows], load_sem.at[2, x]),
-            pltpu.make_async_copy(mass_term.at[rows], v_mass.at[rows], load_sem.at[3, x]),
-        ]
-
-    table_loads = [
-        pltpu.make_async_copy(lane_t, v_lane, load_sem.at[4, 0]),
-        pltpu.make_async_copy(row_t, v_row, load_sem.at[4, 1]),
-    ]
-    late_loads = [
-        pltpu.make_async_copy(right_side, v_rs, load_sem.at[4, 2]),
-        pltpu.make_async_copy(factor, v_fac, load_sem.at[4, 3]),
-        pltpu.make_async_copy(fdm_inverse, v_fdm, load_sem.at[5, 0]),
-    ]
-    for copy in table_loads:
-        copy.start()
-    for x in range(ex):
-        for copy in chunk_loads(x):
-            copy.start()
-    for copy in late_loads:
-        copy.start()
-    for copy in table_loads:
-        copy.wait()
 
     lane_index = lax.broadcasted_iota(jnp.int32, (1, lanes), 1)
     lane_node = lax.rem(lane_index, n)
@@ -385,32 +382,54 @@
     first_line = line_index == 0
     last_line = line_index == n - 1
 
+    for copy in chunk_loads(1):
+        copy.start()
+
     def layers_of(field):
         return [field[k * slab : (k + 1) * slab] for k in range(n)]
 
-    def local_chunk(x, carry):
-        for copy in chunk_loads(x):
+    def load_chunk(x):
+        for copy in chunk_loads(x) + (table_loads(0) if x == 0 else []):
             copy.wait()
-        rows = chunk_rows(x)
+        if x + 2 < ex:
+            for copy in chunk_loads(x + 2):
+                copy.start()
+        elif x + 2 == ex:
+            late_loads[0].start()
+        else:
+            for copy in late_loads[1:]:
+                copy.start()
+
+    def fluxes(x):
+        rows = pl.ds(x * chunk, chunk)
         field = v_adj[rows]
         diffusion = v_con[rows]
         third = diffusion * lane_operator(v_lane[0], field) + v_vel[2, rows] * field
-        total = lane_operator(v_lane[1], third)
         second = diffusion * row_operator(v_row[0], field) + v_vel[1, rows] * field
-        total = total + row_operator(v_row[1], second)
         gradient = jnp.concatenate(odd_operator(derivative, layers_of(field)), axis=0)
         first = diffusion * gradient + v_vel[0, rows] * field
+        return first, second, third
+
+    def divergence(x, first, second, third):
+        rows = pl.ds(x * chunk, chunk)
+        total = lane_operator(v_lane[1], third) + row_operator(v_row[1], second)
         total = total + jnp.concatenate(
             odd_operator(transpose_list(derivative), layers_of(first)), axis=0
         )
-        total = total + v_mass[rows] * field
+        total = total + v_mass[rows] * v_adj[rows]
         crossed = jnp.where(
             is_upper, pltpu.roll(total, lanes - 1, axis=1), pltpu.roll(total, 1, axis=1)
         )
         local[rows] = total + shared * crossed
-        return carry
-
-    lax.fori_loop(0, ex, local_chunk, 0)
+
+    earlier = None
+    for x in range(ex):
+        load_chunk(x)
+        current = fluxes(x)
+        if x > 0:
+            divergence(x - 1, *earlier)
+        earlier = current
+    divergence(ex - 1, *earlier)
 
     low_g = jnp.where(group > 0, 1.0, 0.0).astype(jnp.float32)
     high_g = jnp.where(group < lay.groups - 1, 1.0, 0.0).astype(jnp.float32)
@@ -441,7 +460,7 @@
             )
         return copies
 
-    def send_faces(field, phase):
+    def pack_faces(field, phase):
         side_send[phase, 0] = field[pl.ds(0, slab)]
         side_send[phase, 1] = field[pl.ds(lay.rows - slab, slab)]
         for x in range(ex - 1):
@@ -452,6 +471,8 @@
         for x in range(ex):
             row_send[phase, 0, x] = field[pl.ds(x * chunk, n, stride=slab)]
             row_send[phase, 1, x] = field[pl.ds(x * chunk + slab - 1, n, stride=slab)]
+
+    def send_faces(phase):
         copies = face_copies(phase)
         for copy in copies:
             copy.start()
@@ -483,26 +504,118 @@
         field[starts] = (lower + from_below).reshape(lines * ey, lanes)
         field[ends] = (upper + from_above).reshape(lines * ey, lanes)
 
+    def line_sum(start):
+        total = column_sum[pl.ds(start, ey, stride=n)]
+        for j in range(1, n):
+            total = total + column_sum[pl.ds(start + j, ey, stride=n)]
+        return total
+
+    def joined_sum(start):
+        lower = column_sum[pl.ds(start, ey, stride=n)]
+        upper = column_sum[pl.ds(start + n - 1, ey, stride=n)]
+        below = jnp.where(first_line, 0.0, pltpu.roll(upper, 1, axis=0))
+        above = jnp.where(last_line, 0.0, pltpu.roll(lower, ey - 1, axis=0))
+        return line_sum(start) + below + above
+
+    pack_faces(local, 0)
+    for side in range(2):
+        column_sum[pl.ds(side * slab, slab)] = side_send[0, side]
+    for side in range(2):
+        note_send[side] = joined_sum(side * slab)
+    base = 2 * slab
+    for x in range(ex):
+        layers = layers_of(local[pl.ds(x * chunk, chunk)])
+        total = layers[0]
+        for layer in layers[1:]:
+            total = total + layer
+        column_sum[pl.ds(base + x * slab, slab)] = total
+    for x in range(ex):
+        start = base + x * slab
+        sum_tile[x] = joined_sum(start)
+        note_send[2, pl.ds(x, 1)] = column_sum[pl.ds(start, 1)]
+        note_send[3, pl.ds(x, 1)] = column_sum[pl.ds(start + slab - 1, 1)]
+    for side_g in range(2):
+        for side_d in range(2):
+            spot = side_g * slab + side_d * (slab - 1)
+            note_send[4 + 2 * side_g + side_d] = jnp.broadcast_to(
+                column_sum[pl.ds(spot, 1)], (ey, lanes)
+            )
+    def note_slot(g, d):
+        if d == 0:
+            return (g + 1) // 2
+        if g == 0:
+            return 2 + (d + 1) // 2
+        return 4 + 2 * ((g + 1) // 2) + (d + 1) // 2
+
+    note_copies = [
+        pltpu.make_async_remote_copy(
+            src_ref=note_send.at[note_slot(g, d)],
+            dst_ref=note_recv.at[note_slot(-g, -d)],
+            send_sem=note_sent.at[index],
+            recv_sem=note_got.at[index],
+            device_id=neighbour(g, d),
+            device_id_type=MESH_IDS,
+        )
+        for index, (g, d) in enumerate(steps)
+    ]
+
     pl.semaphore_wait(barrier, len(steps) + lay.pack - 1 + lay.far - 1)
-    first_copies = send_faces(local, 0)
-    for copy in late_loads:
-        copy.wait()
-    join_faces(local, 0, first_copies)
-
+    for copy in note_copies:
+        copy.start()
+    first_copies = send_faces(0)
+    late_loads[0].wait()
     for x in range(ex):
-        rows = pl.ds(x * chunk, chunk)
-        value = v_rs[rows] - local[rows]
-        residual[rows] = value
-        layers = layers_of(value)
+        layers = layers_of(v_rs[pl.ds(x * chunk, chunk)])
         total = layers[0]
         for layer in layers[1:]:
             total = total + layer
         column_sum[pl.ds(x * slab, slab)] = total
-    summed = column_sum[pl.ds(0, columns, stride=n)]
-    for j in range(1, n):
-        summed = summed + column_sum[pl.ds(j, columns, stride=n)]
-    means = jnp.sum(summed, axis=1, keepdims=True) * (1.0 / float(n * n * lanes))
-    means = jnp.broadcast_to(means, (columns, lanes))
+    for x in range(ex):
+        sum_tile[x] = line_sum(x * slab) - sum_tile[x]
+    late_loads[1].wait()
+    def rim_block(line, carry):
+        spot = pl.ds(pl.multiple_of(line * lanes, lanes), lanes)
+        for x in range(ex):
+            rim_send[0, line, pl.ds(x, 1)] = v_fac[pl.ds(x * ey, 1), spot]
+            rim_send[1, line, pl.ds(x, 1)] = v_fac[pl.ds(x * ey + ey - 1, 1), spot]
+        return carry
+
+    lax.fori_loop(0, lay.coarse_lines, rim_block, 0)
+
+    rim_copies = [
+        pltpu.make_async_remote_copy(
+            src_ref=rim_send.at[(d + 1) // 2],
+            dst_ref=rim_recv.at[(1 - d) // 2],
+            send_sem=rim_sem.at[0, (d + 1) // 2],
+            recv_sem=rim_sem.at[1, (d + 1) // 2],
+            device_id=neighbour(0, d),
+            device_id_type=MESH_IDS,
+        )
+        for d in (-1, 1)
+    ]
+    for copy in rim_copies:
+        copy.start()
+    for copy in note_copies:
+        copy.wait_recv()
+    sums = []
+    for x in range(ex):
+        total = sum_tile[x]
+        ends = []
+        for d in range(2):
+            end = note_recv[2 + d, pl.ds(x, ey, stride=0)]
+            if x == 0:
+                end = end + low_g * note_recv[4 + d]
+            if x == ex - 1:
+                end = end + high_g * note_recv[6 + d]
+            ends.append(gates_d[d] * end)
+        if x == 0:
+            total = total - low_g * note_recv[0]
+        if x == ex - 1:
+            total = total - high_g * note_recv[1]
+        total = total - jnp.where(first_line, ends[0], 0.0) - jnp.where(last_line, ends[1], 0.0)
+        sums.append(total)
+    means = jnp.sum(jnp.concatenate(sums, axis=0), axis=1, keepdims=True)
+    means = jnp.broadcast_to(means * (1.0 / float(n * n * lanes)), (columns, lanes))
 
     def inner_block(block, carry):
         for k in range(8):
@@ -545,108 +658,138 @@
     exchange(0, lay.pack, near_id, near_device, lambda index: near_src.at[index], near_in)
     near_in[near_id] = near_src[near_id]
 
-    def solve_chunk(x, carry):
-        rows = chunk_rows(x)
+    join_faces(local, 0, first_copies)
+    for x in range(ex):
+        rows = pl.ds(x * chunk, chunk)
+        residual[rows] = v_rs[rows] - local[rows]
+
+    for copy in late_loads[2:]:
+        copy.wait()
+
+    def solve_chunk(x):
+        rows = pl.ds(x * chunk, chunk)
         field = jnp.concatenate(to_modes(vectors, layers_of(residual[rows])), axis=0)
         field = row_operator(v_row[2], field)
         field = lane_operator(v_lane[2], field) * v_fdm[rows]
         field = lane_operator(v_lane[3], field)
         field = row_operator(v_row[3], field)
         correction[rows] = jnp.concatenate(from_modes(vectors, layers_of(field)), axis=0)
-        return carry
-
-    third = ex // 2
-    lax.fori_loop(0, third, solve_chunk, 0)
+
+    for x in range(ex // 2):
+        solve_chunk(x)
 
     await_exchange(0, lay.pack, near_in, sum_recv)
     far_in[far_id] = jnp.sum(near_in[...], axis=0)
     exchange(1, lay.far, far_id, far_device, lambda index: far_in.at[far_id], far_in)
 
-    lax.fori_loop(third, ex, solve_chunk, 0)
-    second_copies = send_faces(correction, 1)
+    for x in range(ex // 2, ex):
+        solve_chunk(x)
+    pack_faces(correction, 1)
+    second_copies = send_faces(1)
 
     await_exchange(1, lay.far, far_in, sum_recv)
     full_in[near_id] = jnp.sum(far_in[...], axis=0)
     exchange(2, lay.pack, near_id, near_device, lambda index: full_in.at[near_id], full_in)
 
-    join_faces(correction, 1, second_copies)
+    for copy in rim_copies:
+        copy.wait_recv()
 
     await_exchange(2, lay.pack, full_in, sum_recv)
 
-    def value_block(index, total):
+    def value_block(index, totals):
+        inside, left, right = totals
         for k in range(lay.share):
             line = index * lay.share + k
             value = jnp.broadcast_to(full_in[index, pl.ds(k, 1)], (columns, lanes))
-            total = total + v_fac[:, pl.ds(pl.multiple_of(line * lanes, lanes), lanes)] * value
-        return total
-
-    totals = lax.fori_loop(0, lay.pack, value_block, jnp.zeros((columns, lanes), jnp.float32))
-    values = jnp.broadcast_to(jnp.sum(totals, axis=1, keepdims=True), (columns, lanes))
-    own_coarse[...] = values.reshape(ex, ey, lanes)
-
-    ring_copies = []
-    for index, (g, d) in enumerate(steps):
-        x = 0 if g < 0 else ex - 1
-        if d == 0:
-            source, target = own_coarse.at[x], ring_x.at[(1 - g) // 2]
-        elif g == 0:
-            source, target = own_coarse, ring_y.at[(1 - d) // 2]
-        else:
-            source, target = own_coarse.at[x], ring_d.at[(1 - g) // 2, (1 - d) // 2]
-        copy = pltpu.make_async_remote_copy(
-            src_ref=source,
-            dst_ref=target,
-            send_sem=ring_send.at[index],
-            recv_sem=ring_recv.at[index],
-            device_id=neighbour(g, d),
+            spot = pl.ds(pl.multiple_of(line * lanes, lanes), lanes)
+            inside = inside + v_fac[:, spot] * value
+            left = left + rim_recv[0, line] * value[:ex]
+            right = right + rim_recv[1, line] * value[:ex]
+        return inside, left, right
+
+    none = jnp.zeros((ex, lanes), jnp.float32)
+    inside, left, right = lax.fori_loop(
+        0, lay.pack, value_block, (jnp.zeros((columns, lanes), jnp.float32), none, none)
+    )
+    inside = jnp.broadcast_to(jnp.sum(inside, axis=1, keepdims=True), (columns, lanes))
+    left = low_d * jnp.sum(left, axis=1, keepdims=True)
+    right = high_d * jnp.sum(right, axis=1, keepdims=True)
+    for x in range(ex):
+        grid[0, 1 + x] = inside[x * ey : (x + 1) * ey]
+        grid[1, 1 + x] = jnp.broadcast_to(left[x : x + 1], (ey, lanes))
+        grid[2, 1 + x] = jnp.broadcast_to(right[x : x + 1], (ey, lanes))
+    for part in range(3):
+        ring_out[0, part] = grid[part, 1]
+        ring_out[1, part] = grid[part, ex]
+    ring_copies = [
+        pltpu.make_async_remote_copy(
+            src_ref=ring_out.at[(g + 1) // 2],
+            dst_ref=ring_in.at[(1 - g) // 2],
+            send_sem=ring_sem.at[0, (g + 1) // 2],
+            recv_sem=ring_sem.at[1, (g + 1) // 2],
+            device_id=neighbour(g, 0),
             device_id_type=MESH_IDS,
         )
+        for g in (-1, 1)
+    ]
+    for copy in ring_copies:
         copy.start()
-        ring_copies.append(copy)
+    join_faces(correction, 1, second_copies)
     for copy in ring_copies:
         copy.wait_recv()
-
-    def padded(inside, below, above):
-        return [low_g * below] + inside + [high_g * above]
-
-    center = padded([own_coarse[x] for x in range(ex)], ring_x[0], ring_x[1])
-    left = padded([ring_y[0, x] for x in range(ex)], ring_d[0, 0], ring_d[1, 0])
-    right = padded([ring_y[1, x] for x in range(ex)], ring_d[0, 1], ring_d[1, 1])
-    twice = 1.0 + shared
+    for part in range(3):
+        grid[part, 0] = low_g * ring_in[0, part]
+        grid[part, ex + 1] = high_g * ring_in[1, part]
+
+    for copy in note_copies + first_copies + rim_copies + second_copies + ring_copies:
+        copy.wait_send()
+    await_exchange(0, lay.pack, near_in, sum_send)
+    await_exchange(1, lay.far, far_in, sum_send)
+    await_exchange(2, lay.pack, full_in, sum_send)
+
+
+def finish_kernel(lay, residual, solved, grid, out_residual, out_correction, staged, tile, sem):
+    ex, n, ey, lanes, slab, chunk = lay.ex, lay.n, lay.ey, lay.lanes, lay.slab, lay.chunk
+    copies = [pltpu.make_async_copy(residual, out_residual, sem.at[0])]
+    copies[0].start()
+    lane_index = lax.broadcasted_iota(jnp.int32, (1, lanes), 1)
+    lane_node = lax.rem(lane_index, n)
+    shared = ((lane_node == n - 1) & (lane_index != lanes - 1)) | (
+        (lane_node == 0) & (lane_index != 0)
+    )
+    copies_of = jnp.where(shared, 2.0, 1.0).astype(jnp.float32)
+    line_index = lax.broadcasted_iota(jnp.int32, (ey, lanes), 0)
+    first_line, last_line = line_index == 0, line_index == ey - 1
     for x in range(ex):
-        rows = x * chunk
         for part in range(3):
-            def joined(values):
-                value = values[x + 1]
+            sides = []
+            for side in range(3):
+                value = grid[side, x + 1]
                 if part == 0:
-                    value = value + values[x]
+                    value = value + grid[side, x]
                 elif part == 2:
-                    value = value + values[x + 2]
-                return value * twice
-
-            inside = joined(center)
-            before = low_d * pltpu.roll(joined(left), 1, axis=0)
-            after = high_d * pltpu.roll(joined(right), ey - 1, axis=0)
-            below = jnp.where(first_line, before, pltpu.roll(inside, 1, axis=0))
-            above = jnp.where(last_line, after, pltpu.roll(inside, ey - 1, axis=0))
+                    value = value + grid[side, x + 2]
+                sides.append(value * copies_of)
+            inside, left, right = sides
+            below = jnp.where(first_line, left, pltpu.roll(inside, 1, axis=0))
+            above = jnp.where(last_line, right, pltpu.roll(inside, ey - 1, axis=0))
             for j in range(n):
                 value = inside
                 if j == 0:
                     value = inside + below
                 elif j == n - 1:
                     value = inside + above
-                coarse_tile[part, pl.ds(j, ey, stride=n)] = value
-            layers = {0: [0], 1: list(range(1, n - 1)), 2: [n - 1]}[part]
-            tile = coarse_tile[part]
-            for layer in layers:
-                spot = pl.ds(rows + layer * slab, slab)
-                correction[spot] = correction[spot] + tile
-
-    for copy in first_copies + second_copies + ring_copies:
-        copy.wait_send()
-    await_exchange(0, lay.pack, near_in, sum_send)
-    await_exchange(1, lay.far, far_in, sum_send)
-    await_exchange(2, lay.pack, full_in, sum_send)
+                tile[x, part, pl.ds(j, ey, stride=n)] = value
+        for layer in range(n):
+            part = 0 if layer == 0 else 2 if layer == n - 1 else 1
+            spot = pl.ds(x * chunk + layer * slab, slab)
+            staged[spot] = solved[spot] + tile[x, part]
+        rows = pl.ds(x * chunk, chunk)
+        copy = pltpu.make_async_copy(staged.at[rows], out_correction.at[rows], sem.at[1 + x])
+        copy.start()
+        copies.append(copy)
+    for copy in copies:
+        copy.wait()
 
 
 def solution(mesh):
@@ -658,7 +801,7 @@
         derivative, vectors, lane_tables, row_tables = operator_tables(n, lanes)
         flat = (lay.rows, lanes)
         f32, bf16 = jnp.float32, jnp.bfloat16
-        anywhere = pl.BlockSpec(memory_space=pltpu.HBM)
+        hbm = pl.BlockSpec(memory_space=pltpu.HBM)
         vmem = pl.BlockSpec(memory_space=pltpu.VMEM)
         scratch = [
             pltpu.VMEM(flat, f32),
@@ -677,31 +820,39 @@
             pltpu.VMEM((2, 2, ex, n, lanes), f32),
             pltpu.VMEM((2, 2, 2, n, lanes), f32),
             pltpu.VMEM((lay.lines * ey, lanes), f32),
-            pltpu.VMEM((ex * lay.slab, lanes), f32),
+            pltpu.VMEM(((2 + ex) * lay.slab, lanes), f32),
             pltpu.VMEM((lay.coarse_lines * 8, lanes), f32),
             pltpu.VMEM((lay.pack, lay.share, lanes), f32),
             pltpu.VMEM((lay.pack, lay.share, lanes), f32),
             pltpu.VMEM((lay.far, lay.share, lanes), f32),
             pltpu.VMEM((lay.pack, lay.share, lanes), f32),
             pltpu.VMEM((ex, ey, lanes), f32),
-            pltpu.VMEM((2, ey, lanes), f32),
-            pltpu.VMEM((2, ex, ey, lanes), f32),
-            pltpu.VMEM((2, 2, ey, lanes), f32),
-            pltpu.VMEM((8, lanes), f32),
-            pltpu.VMEM((3, lay.slab, lanes), f32),
+            pltpu.VMEM((8, ey, lanes), f32),
+            pltpu.VMEM((8, ey, lanes), f32),
+            pltpu.VMEM((2, lay.coarse_lines, ex, lanes), f32),
+            pltpu.VMEM((2, lay.coarse_lines, ex, lanes), f32),
+            pltpu.VMEM((2, 3, ey, lanes), f32),
+            pltpu.VMEM((2, 3, ey, lanes), f32),
             pltpu.SemaphoreType.DMA((6, 4)),
             pltpu.SemaphoreType.DMA((2, 8)),
             pltpu.SemaphoreType.DMA((2, 8)),
             pltpu.SemaphoreType.DMA((8,)),
             pltpu.SemaphoreType.DMA((8,)),
+            pltpu.SemaphoreType.DMA((2, 2)),
+            pltpu.SemaphoreType.DMA((2, 2)),
             pltpu.SemaphoreType.DMA((3,)),
             pltpu.SemaphoreType.DMA((3,)),
         ]
-        residual, correction = pl.pallas_call(
+        grid = (3, ex + 2, ey, lanes)
+        residual, solved, grid_values = pl.pallas_call(
             functools.partial(step_kernel, lay, derivative, vectors),
-            out_shape=[jax.ShapeDtypeStruct(flat, f32)] * 2,
-            in_specs=[anywhere] * 9,
-            out_specs=[vmem, vmem],
+            out_shape=[
+                jax.ShapeDtypeStruct(flat, f32),
+                jax.ShapeDtypeStruct(flat, f32),
+                jax.ShapeDtypeStruct(grid, f32),
+            ],
+            in_specs=[hbm] * 9,
+            out_specs=[vmem] * 3,
             scratch_shapes=scratch,
             compiler_params=pltpu.CompilerParams(
                 collective_id=0, has_side_effects=True, vmem_limit_bytes=40 * 1024 * 1024
@@ -723,6 +874,23 @@
                 )
             ]
         )
+        residual, correction = pl.pallas_call(
+            functools.partial(finish_kernel, lay),
+            out_shape=[pltpu.HBM(flat, f32)] * 2,
+            in_specs=[vmem] * 3,
+            out_specs=[hbm] * 2,
+            scratch_shapes=[
+                pltpu.VMEM(flat, f32),
+                pltpu.VMEM((ex, 3, lay.slab, lanes), f32),
+                pltpu.SemaphoreType.DMA((1 + ex,)),
+            ],
+            name="finish",
+        )(
+            *[
+                pltpu.with_memory_space_constraint(array, pltpu.VMEM)
+                for array in (residual, solved, grid_values)
+            ]
+        )
         return residual.reshape(adjoint.shape), correction.reshape(adjoint.shape)
 
     field = P("grp", None, "dev", None, None)

time: 39.8 us -> 37 us (0.930)
  local copies, waits for them, and re-layouts: 1.94 us -> 0 us
  Pallas kernels: 37.1 us -> 36.3 us
    pallas_call x1, Pallas kernels: 37.1 us -> 34.9 us  [body(): pl.pallas_call(functools.partial(step_kernel, lay, derivative, vectors),...]
    unnamed x2 -> x0, local copies, waits for them, and re-layouts: 1.94 us -> none
    pallas_call x0 -> x1, Pallas kernels: none -> 1.35 us  [body(): pl.pallas_call(functools.partial(finish_kernel, lay), out_shape=[pltpu.HB...]
where the time goes in v2:
time: 37 us; the launch traced here: 36.9 us
  Pallas kernels  36.3 us (98%)
  between operations  0.64 us (2%)
    pallas_call x1, Pallas kernels, body(): pl.pallas_call(functools.partial(step_kernel, lay, derivative, vectors),...  34.9 us
    pallas_call x1, Pallas kernels, body(): pl.pallas_call(functools.partial(finish_kernel, lay), out_shape=[pltpu.HB...  1.35 us

profile of v2, /device:TPU:1, one launch (start us, length us, event | category | flops | bytes accessed | tf_op | source)
XLA Modules:
  0.0 36.9 jit_solution(10613792167637415333)
XLA Ops:
  0.6 34.9 %adjoint_step.1 = (f32[2048,128]{1,0:T(8,128)S(1)}, f32[2048,128]{1,0:T(8,128)S(1)}, f32[3,6,8,128]{3,2,1,0:T(8,128)S(1)}) custom-call(f32[2048,128]{1,0:T(8,128)} %bitcast.9, f32[2048,128]{1,0:T(8,128)} %bitcast.10, f32[3,2048,128]{2,1,0:T(8,128)} %bitcast.8, f32[2048,128]{1,0:T(8,128)} %bitcast.11, f32[2048,128]{1,0:T(8,128)} %bitcast.12, ...), custom_call_target="tpu_custom_call" | custom-call | tf_op jit(solution)/shard_map/adjoint_step/pallas_call | solution.py:847
  35.6 1.4 %finish.1 = (f32[2048,128]{1,0:T(8,128)}, f32[2048,128]{1,0:T(8,128)}) custom-call(f32[2048,128]{1,0:T(8,128)S(1)} %get-tuple-element.7.residual, f32[2048,128]{1,0:T(8,128)S(1)} %get-tuple-element.8.solved, f32[3,6,8,128]{3,2,1,0:T(8,128)S(1)} %get-tuple-element.9.grid), custom_call_target="tpu_custom_call" | custom-call | tf_op jit(solution)/shard_map/finish/pallas_call | solution.py:877

commit v3 on v2

--- a/solution.py
+++ b/solution.py
@@ -305,7 +305,7 @@
     lay, derivative, vectors,
     adjoint, right_side, velocity, conductivity, mass_term, fdm_inverse, factor, lane_t, row_t,
     residual, correction, grid,
-    v_adj, v_rs, v_vel, v_con, v_mass, v_fdm, v_fac, v_lane, v_row,
+    v_adj, v_rs, v_vel, v_con, v_mass, v_fdm, v_fac, v_lane, v_row, flux_sum,
     local, side_send, side_recv, row_send, row_recv, edge_recv, halo_lines,
     column_sum, inner_part, near_src, near_in, far_in, full_in,
     sum_tile, note_send, note_recv, rim_send, rim_recv, ring_out, ring_in,
@@ -361,13 +361,17 @@
     for copy in chunk_loads(0) + table_loads(0):
         copy.start()
 
+    def ring_steps(offset, size):
+        return min(offset % size, -offset % size)
+
+    def near_hops(offset):
+        return ring_steps(offset // 2, 4) + offset // 8
+
+    def far_hops(offset):
+        return 2 * ring_steps(offset // far_blocks, lay.groups) + ring_steps(offset, far_blocks)
+
     barrier = pltpu.get_barrier_semaphore()
-    for step in steps:
-        pl.semaphore_signal(barrier, inc=1, device_id=neighbour(*step), device_id_type=MESH_IDS)
-    for offset in range(1, lay.pack):
-        target = near_device(lax.rem(near_id + offset, lay.pack))
-        pl.semaphore_signal(barrier, inc=1, device_id=target, device_id_type=MESH_IDS)
-    for offset in range(1, lay.far):
+    for offset in sorted(range(1, lay.far), key=far_hops, reverse=True):
         target = far_device(lax.rem(far_id + offset, lay.far))
         pl.semaphore_signal(barrier, inc=1, device_id=target, device_id_type=MESH_IDS)
 
@@ -381,7 +385,11 @@
     line_index = lax.broadcasted_iota(jnp.int32, (n, lanes), 0)
     first_line = line_index == 0
     last_line = line_index == n - 1
-
+    for step in steps:
+        pl.semaphore_signal(barrier, inc=1, device_id=neighbour(*step), device_id_type=MESH_IDS)
+    for offset in range(1, lay.pack):
+        target = near_device(lax.rem(near_id + offset, lay.pack))
+        pl.semaphore_signal(barrier, inc=1, device_id=target, device_id_type=MESH_IDS)
     for copy in chunk_loads(1):
         copy.start()
 
@@ -400,7 +408,16 @@
             for copy in late_loads[1:]:
                 copy.start()
 
-    def fluxes(x):
+    copies_of = 1.0 + shared
+    at_low = [line[0] for line in derivative]
+    at_high = [line[n - 1] for line in derivative]
+    third_weight = jnp.zeros((1, lanes), jnp.float32)
+    for node in range(n):
+        ends = jnp.where(lane_index >= n, at_low[node], 0.0)
+        ends = ends + jnp.where(lane_index < lanes - n, at_high[node], 0.0)
+        third_weight = third_weight + jnp.where(lane_node == node, ends, 0.0)
+
+    def flux_chunk(x):
         rows = pl.ds(x * chunk, chunk)
         field = v_adj[rows]
         diffusion = v_con[rows]
@@ -408,28 +425,55 @@
         second = diffusion * row_operator(v_row[0], field) + v_vel[1, rows] * field
         gradient = jnp.concatenate(odd_operator(derivative, layers_of(field)), axis=0)
         first = diffusion * gradient + v_vel[0, rows] * field
-        return first, second, third
-
-    def divergence(x, first, second, third):
+        mass = v_mass[rows] * field
+        v_vel[0, rows] = first
+        v_vel[1, rows] = second
+        v_vel[2, rows] = third
+        local[rows] = mass
+        first, second, third, mass = [layers_of(value) for value in (first, second, third, mass)]
+
+        def whole(layers):
+            total = layers[0]
+            for layer in layers[1:]:
+                total = total + layer
+            return total
+
+        parts = [
+            (whole(mass), whole(third), whole(second)),
+            (mass[0] + weighted(at_low, first), third[0], second[0]),
+            (mass[n - 1] + weighted(at_high, first), third[n - 1], second[n - 1]),
+        ]
+        for part, (plain, lanewise, linewise) in enumerate(parts):
+            flux_sum[part, x, 0] = copies_of * plain + third_weight * lanewise
+            flux_sum[part, x, 1] = copies_of * linewise
+
+    def divergence(x):
         rows = pl.ds(x * chunk, chunk)
-        total = lane_operator(v_lane[1], third) + row_operator(v_row[1], second)
+        total = lane_operator(v_lane[1], v_vel[2, rows]) + row_operator(v_row[1], v_vel[1, rows])
         total = total + jnp.concatenate(
-            odd_operator(transpose_list(derivative), layers_of(first)), axis=0
+            odd_operator(transpose_list(derivative), layers_of(v_vel[0, rows])), axis=0
         )
-        total = total + v_mass[rows] * v_adj[rows]
+        total = total + local[rows]
         crossed = jnp.where(
             is_upper, pltpu.roll(total, lanes - 1, axis=1), pltpu.roll(total, 1, axis=1)
         )
         local[rows] = total + shared * crossed
 
-    earlier = None
+    def joined_sum(slot):
+        plain = [column_sum[pl.ds(slot * 2 * slab + j, ey, stride=n)] for j in range(n)]
+        linewise = [column_sum[pl.ds((slot * 2 + 1) * slab + j, ey, stride=n)] for j in range(n)]
+        total = plain[0]
+        for value in plain[1:]:
+            total = total + value
+        lower = plain[0] + weighted(at_low, linewise)
+        upper = plain[n - 1] + weighted(at_high, linewise)
+        below = jnp.where(first_line, 0.0, pltpu.roll(upper, 1, axis=0))
+        above = jnp.where(last_line, 0.0, pltpu.roll(lower, ey - 1, axis=0))
+        return total + below + above, lower, upper
+
     for x in range(ex):
         load_chunk(x)
-        current = fluxes(x)
-        if x > 0:
-            divergence(x - 1, *earlier)
-        earlier = current
-    divergence(ex - 1, *earlier)
+        flux_chunk(x)
 
     low_g = jnp.where(group > 0, 1.0, 0.0).astype(jnp.float32)
     high_g = jnp.where(group < lay.groups - 1, 1.0, 0.0).astype(jnp.float32)
@@ -504,42 +548,47 @@
         field[starts] = (lower + from_below).reshape(lines * ey, lanes)
         field[ends] = (upper + from_above).reshape(lines * ey, lanes)
 
-    def line_sum(start):
-        total = column_sum[pl.ds(start, ey, stride=n)]
-        for j in range(1, n):
-            total = total + column_sum[pl.ds(start + j, ey, stride=n)]
-        return total
-
-    def joined_sum(start):
-        lower = column_sum[pl.ds(start, ey, stride=n)]
-        upper = column_sum[pl.ds(start + n - 1, ey, stride=n)]
-        below = jnp.where(first_line, 0.0, pltpu.roll(upper, 1, axis=0))
-        above = jnp.where(last_line, 0.0, pltpu.roll(lower, ey - 1, axis=0))
-        return line_sum(start) + below + above
-
-    pack_faces(local, 0)
+    for part in range(2):
+        column_sum[pl.ds(part * slab, slab)] = flux_sum[1, 0, part]
+        column_sum[pl.ds((2 + part) * slab, slab)] = flux_sum[2, ex - 1, part]
+        for x in range(ex):
+            total = flux_sum[0, x, part]
+            if x > 0:
+                total = total + flux_sum[2, x - 1, part]
+            if x < ex - 1:
+                total = total + flux_sum[1, x + 1, part]
+            column_sum[pl.ds((4 + 2 * x + part) * slab, slab)] = total
     for side in range(2):
-        column_sum[pl.ds(side * slab, slab)] = side_send[0, side]
-    for side in range(2):
-        note_send[side] = joined_sum(side * slab)
-    base = 2 * slab
+        total, lower, upper = joined_sum(side)
+        note_send[side] = total
+        note_send[4 + 2 * side] = jnp.broadcast_to(lower[0:1], (ey, lanes))
+        note_send[5 + 2 * side] = jnp.broadcast_to(upper[ey - 1 : ey], (ey, lanes))
     for x in range(ex):
-        layers = layers_of(local[pl.ds(x * chunk, chunk)])
-        total = layers[0]
-        for layer in layers[1:]:
-            total = total + layer
-        column_sum[pl.ds(base + x * slab, slab)] = total
-    for x in range(ex):
-        start = base + x * slab
-        sum_tile[x] = joined_sum(start)
-        note_send[2, pl.ds(x, 1)] = column_sum[pl.ds(start, 1)]
-        note_send[3, pl.ds(x, 1)] = column_sum[pl.ds(start + slab - 1, 1)]
-    for side_g in range(2):
-        for side_d in range(2):
-            spot = side_g * slab + side_d * (slab - 1)
-            note_send[4 + 2 * side_g + side_d] = jnp.broadcast_to(
-                column_sum[pl.ds(spot, 1)], (ey, lanes)
-            )
+        total, lower, upper = joined_sum(2 + x)
+        sum_tile[x] = total
+        note_send[2, pl.ds(x, 1)] = lower[0:1]
+        note_send[3, pl.ds(x, 1)] = upper[ey - 1 : ey]
+
+    def exists(g, d):
+        found = (group + g >= 0) & (group + g < lay.groups)
+        return found & (device + d >= 0) & (device + d < lay.devices)
+
+    def start_inside(copies, ways):
+        for copy, (g, d) in zip(copies, ways):
+            pl.when(exists(g, d))(copy.start)
+
+    def await_inside(copies, ways):
+        for copy, (g, d) in zip(copies, ways):
+            pl.when(exists(-g, -d))(copy.wait_recv)
+
+    def await_sent(copies, ways):
+        for copy, (g, d) in zip(copies, ways):
+            pl.when(exists(g, d))(copy.wait_send)
+
+    whole_line = jnp.zeros((n, lanes), jnp.int32)
+    has_low_g, has_high_g = whole_line + group > 0, whole_line + group < lay.groups - 1
+    has_low_d, has_high_d = whole_line + device > 0, whole_line + device < lay.devices - 1
+
     def note_slot(g, d):
         if d == 0:
             return (g + 1) // 2
@@ -560,9 +609,7 @@
     ]
 
     pl.semaphore_wait(barrier, len(steps) + lay.pack - 1 + lay.far - 1)
-    for copy in note_copies:
-        copy.start()
-    first_copies = send_faces(0)
+    start_inside(note_copies, steps)
     late_loads[0].wait()
     for x in range(ex):
         layers = layers_of(v_rs[pl.ds(x * chunk, chunk)])
@@ -571,7 +618,10 @@
             total = total + layer
         column_sum[pl.ds(x * slab, slab)] = total
     for x in range(ex):
-        sum_tile[x] = line_sum(x * slab) - sum_tile[x]
+        total = column_sum[pl.ds(x * slab, ey, stride=n)]
+        for j in range(1, n):
+            total = total + column_sum[pl.ds(x * slab + j, ey, stride=n)]
+        sum_tile[x] = total - sum_tile[x]
     late_loads[1].wait()
     def rim_block(line, carry):
         spot = pl.ds(pl.multiple_of(line * lanes, lanes), lanes)
@@ -595,8 +645,11 @@
     ]
     for copy in rim_copies:
         copy.start()
-    for copy in note_copies:
-        copy.wait_recv()
+    for x in range(ex):
+        divergence(x)
+    pack_faces(local, 0)
+    first_copies = send_faces(0)
+    await_inside(note_copies, steps)
     sums = []
     for x in range(ex):
         total = sum_tile[x]
@@ -604,14 +657,14 @@
         for d in range(2):
             end = note_recv[2 + d, pl.ds(x, ey, stride=0)]
             if x == 0:
-                end = end + low_g * note_recv[4 + d]
+                end = end + jnp.where(has_low_g, note_recv[4 + d], 0.0)
             if x == ex - 1:
-                end = end + high_g * note_recv[6 + d]
-            ends.append(gates_d[d] * end)
+                end = end + jnp.where(has_high_g, note_recv[6 + d], 0.0)
+            ends.append(jnp.where((has_low_d, has_high_d)[d], end, 0.0))
         if x == 0:
-            total = total - low_g * note_recv[0]
+            total = total - jnp.where(has_low_g, note_recv[0], 0.0)
         if x == ex - 1:
-            total = total - high_g * note_recv[1]
+            total = total - jnp.where(has_high_g, note_recv[1], 0.0)
         total = total - jnp.where(first_line, ends[0], 0.0) - jnp.where(last_line, ends[1], 0.0)
         sums.append(total)
     means = jnp.sum(jnp.concatenate(sums, axis=0), axis=1, keepdims=True)
@@ -648,7 +701,7 @@
             ).start()
             return carry
 
-        for offset in range(1, count):
+        for offset in sorted(range(1, count), key=far_hops if stage == 1 else near_hops, reverse=True):
             send(offset, 0)
 
     def await_exchange(stage, count, buffer, sem):
@@ -657,6 +710,11 @@
 
     exchange(0, lay.pack, near_id, near_device, lambda index: near_src.at[index], near_in)
     near_in[near_id] = near_src[near_id]
+
+
+    await_exchange(0, lay.pack, near_in, sum_recv)
+    far_in[far_id] = jnp.sum(near_in[...], axis=0)
+    exchange(1, lay.far, far_id, far_device, lambda index: far_in.at[far_id], far_in)
 
     join_faces(local, 0, first_copies)
     for x in range(ex):
@@ -675,14 +733,7 @@
         field = row_operator(v_row[3], field)
         correction[rows] = jnp.concatenate(from_modes(vectors, layers_of(field)), axis=0)
 
-    for x in range(ex // 2):
-        solve_chunk(x)
-
-    await_exchange(0, lay.pack, near_in, sum_recv)
-    far_in[far_id] = jnp.sum(near_in[...], axis=0)
-    exchange(1, lay.far, far_id, far_device, lambda index: far_in.at[far_id], far_in)
-
-    for x in range(ex // 2, ex):
+    for x in range(ex):
         solve_chunk(x)
     pack_faces(correction, 1)
     second_copies = send_faces(1)
@@ -732,16 +783,17 @@
         )
         for g in (-1, 1)
     ]
-    for copy in ring_copies:
-        copy.start()
+    ring_ways = [(-1, 0), (1, 0)]
+    start_inside(ring_copies, ring_ways)
     join_faces(correction, 1, second_copies)
-    for copy in ring_copies:
-        copy.wait_recv()
+    await_inside(ring_copies, ring_ways)
     for part in range(3):
-        grid[part, 0] = low_g * ring_in[0, part]
-        grid[part, ex + 1] = high_g * ring_in[1, part]
-
-    for copy in note_copies + first_copies + rim_copies + second_copies + ring_copies:
+        grid[part, 0] = jnp.where(has_low_g, ring_in[0, part], 0.0)
+        grid[part, ex + 1] = jnp.where(has_high_g, ring_in[1, part], 0.0)
+
+    await_sent(note_copies, steps)
+    await_sent(ring_copies, ring_ways)
+    for copy in first_copies + rim_copies + second_copies:
         copy.wait_send()
     await_exchange(0, lay.pack, near_in, sum_send)
     await_exchange(1, lay.far, far_in, sum_send)
@@ -813,6 +865,7 @@
             pltpu.VMEM(coarse_factor.shape, f32),
             pltpu.VMEM(lane_tables.shape, bf16),
             pltpu.VMEM(row_tables.shape, bf16),
+            pltpu.VMEM((3, ex, 2, lay.slab, lanes), f32),
             pltpu.VMEM(flat, f32),
             pltpu.VMEM((2, 2, lay.slab, lanes), f32),
             pltpu.VMEM((2, 2, lay.slab, lanes), f32),
@@ -820,7 +873,7 @@
             pltpu.VMEM((2, 2, ex, n, lanes), f32),
             pltpu.VMEM((2, 2, 2, n, lanes), f32),
             pltpu.VMEM((lay.lines * ey, lanes), f32),
-            pltpu.VMEM(((2 + ex) * lay.slab, lanes), f32),
+            pltpu.VMEM((2 * (2 + ex) * lay.slab, lanes), f32),
             pltpu.VMEM((lay.coarse_lines * 8, lanes), f32),
             pltpu.VMEM((lay.pack, lay.share, lanes), f32),
             pltpu.VMEM((lay.pack, lay.share, lanes), f32),

time: 37 us -> 35.1 us (0.949)
  Pallas kernels: 36.3 us -> 34.3 us
    pallas_call x1, Pallas kernels: 34.9 us -> 32.9 us  [body(): pl.pallas_call(functools.partial(step_kernel, lay, derivative, vectors),...]
where the time goes in v3:
time: 35.1 us; the launch traced here: 34.9 us
  Pallas kernels  34.3 us (98%)
  between operations  0.64 us (2%)
    pallas_call x1, Pallas kernels, body(): pl.pallas_call(functools.partial(step_kernel, lay, derivative, vectors),...  32.9 us
    pallas_call x1, Pallas kernels, body(): pl.pallas_call(functools.partial(finish_kernel, lay), out_shape=[pltpu.HB...  1.35 us

profile of v3, /device:TPU:1, one launch (start us, length us, event | category | flops | bytes accessed | tf_op | source)
XLA Modules:
  0.0 34.9 jit_solution(4821928168089222164)
XLA Ops:
  0.6 32.9 %adjoint_step.1 = (f32[2048,128]{1,0:T(8,128)S(1)}, f32[2048,128]{1,0:T(8,128)S(1)}, f32[3,6,8,128]{3,2,1,0:T(8,128)S(1)}) custom-call(f32[2048,128]{1,0:T(8,128)} %bitcast.9, f32[2048,128]{1,0:T(8,128)} %bitcast.10, f32[3,2048,128]{2,1,0:T(8,128)} %bitcast.8, f32[2048,128]{1,0:T(8,128)} %bitcast.11, f32[2048,128]{1,0:T(8,128)} %bitcast.12, ...), custom_call_target="tpu_custom_call" | custom-call | tf_op jit(solution)/shard_map/adjoint_step/pallas_call | solution.py:900
  33.6 1.4 %finish.1 = (f32[2048,128]{1,0:T(8,128)}, f32[2048,128]{1,0:T(8,128)}) custom-call(f32[2048,128]{1,0:T(8,128)S(1)} %get-tuple-element.7.residual, f32[2048,128]{1,0:T(8,128)S(1)} %get-tuple-element.8.solved, f32[3,6,8,128]{3,2,1,0:T(8,128)S(1)} %get-tuple-element.9.grid), custom_call_target="tpu_custom_call" | custom-call | tf_op jit(solution)/shard_map/finish/pallas_call | solution.py:930

commit v4 on v3

--- a/solution.py
+++ b/solution.py
@@ -475,12 +475,6 @@
         load_chunk(x)
         flux_chunk(x)
 
-    low_g = jnp.where(group > 0, 1.0, 0.0).astype(jnp.float32)
-    high_g = jnp.where(group < lay.groups - 1, 1.0, 0.0).astype(jnp.float32)
-    low_d = jnp.where(device > 0, 1.0, 0.0).astype(jnp.float32)
-    high_d = jnp.where(device < lay.devices - 1, 1.0, 0.0).astype(jnp.float32)
-    gates_g, gates_d = (low_g, high_g), (low_d, high_d)
-
     def face_copies(phase):
         copies = []
         for index, (g, d) in enumerate(steps):
@@ -518,26 +512,27 @@
 
     def send_faces(phase):
         copies = face_copies(phase)
-        for copy in copies:
-            copy.start()
+        start_inside(copies, steps)
         return copies
 
     def join_faces(field, phase, copies):
-        for copy in copies:
-            copy.wait_recv()
+        await_inside(copies, steps)
+        whole_slab = jnp.zeros((slab, lanes), jnp.int32)
         head, tail = pl.ds(0, slab), pl.ds(lay.rows - slab, slab)
-        field[head] = field[head] + low_g * side_recv[phase, 0]
-        field[tail] = field[tail] + high_g * side_recv[phase, 1]
+        field[head] = field[head] + jnp.where(whole_slab + group > 0, side_recv[phase, 0], 0.0)
+        beyond = jnp.where(whole_slab + group < lay.groups - 1, side_recv[phase, 1], 0.0)
+        field[tail] = field[tail] + beyond
         for d in range(2):
             low_edge = edge_recv[phase, 0, d, pl.ds(n - 1, n, stride=0)]
             high_edge = edge_recv[phase, 1, d, pl.ds(0, n, stride=0)]
-            first = row_recv[phase, d, 0] + jnp.where(first_line, low_g * low_edge, 0.0)
+            first = row_recv[phase, d, 0] + jnp.where(first_line & has_low_g, low_edge, 0.0)
             row_recv[phase, d, 0] = first
-            last = row_recv[phase, d, ex - 1] + jnp.where(last_line, high_g * high_edge, 0.0)
+            last = row_recv[phase, d, ex - 1] + jnp.where(last_line & has_high_g, high_edge, 0.0)
             row_recv[phase, d, ex - 1] = last
             spot = 0 if d == 0 else n - 1
             for x in range(ex):
-                halo_lines[pl.ds(x * slab + spot, n, stride=n)] = gates_d[d] * row_recv[phase, d, x]
+                outer = jnp.where((has_low_d, has_high_d)[d], row_recv[phase, d, x], 0.0)
+                halo_lines[pl.ds(x * slab + spot, n, stride=n)] = outer
         starts = pl.ds(0, lines * ey, stride=n)
         ends = pl.ds(n - 1, lines * ey, stride=n)
         lower = field[starts].reshape(lines, ey, lanes)
@@ -643,8 +638,8 @@
         )
         for d in (-1, 1)
     ]
-    for copy in rim_copies:
-        copy.start()
+    rim_ways = [(0, -1), (0, 1)]
+    start_inside(rim_copies, rim_ways)
     for x in range(ex):
         divergence(x)
     pack_faces(local, 0)
@@ -742,8 +737,7 @@
     full_in[near_id] = jnp.sum(far_in[...], axis=0)
     exchange(2, lay.pack, near_id, near_device, lambda index: full_in.at[near_id], full_in)
 
-    for copy in rim_copies:
-        copy.wait_recv()
+    await_inside(rim_copies, rim_ways)
 
     await_exchange(2, lay.pack, full_in, sum_recv)
 
@@ -763,8 +757,9 @@
         0, lay.pack, value_block, (jnp.zeros((columns, lanes), jnp.float32), none, none)
     )
     inside = jnp.broadcast_to(jnp.sum(inside, axis=1, keepdims=True), (columns, lanes))
-    left = low_d * jnp.sum(left, axis=1, keepdims=True)
-    right = high_d * jnp.sum(right, axis=1, keepdims=True)
+    rim_line = jnp.zeros((ex, 1), jnp.int32) + device
+    left = jnp.where(rim_line > 0, jnp.sum(left, axis=1, keepdims=True), 0.0)
+    right = jnp.where(rim_line < lay.devices - 1, jnp.sum(right, axis=1, keepdims=True), 0.0)
     for x in range(ex):
         grid[0, 1 + x] = inside[x * ey : (x + 1) * ey]
         grid[1, 1 + x] = jnp.broadcast_to(left[x : x + 1], (ey, lanes))
@@ -793,8 +788,9 @@
 
     await_sent(note_copies, steps)
     await_sent(ring_copies, ring_ways)
-    for copy in first_copies + rim_copies + second_copies:
-        copy.wait_send()
+    await_sent(first_copies, steps)
+    await_sent(rim_copies, rim_ways)
+    await_sent(second_copies, steps)
     await_exchange(0, lay.pack, near_in, sum_send)
     await_exchange(1, lay.far, far_in, sum_send)
     await_exchange(2, lay.pack, full_in, sum_send)

time: 35.1 us -> 35 us (level)
  no operation moved by 1% of the time
where the time goes in v4:
time: 35 us; the launch traced here: 34.9 us
  Pallas kernels  34.3 us (98%)
  between operations  0.64 us (2%)
    pallas_call x1, Pallas kernels, body(): pl.pallas_call(functools.partial(step_kernel, lay, derivative, vectors),...  32.9 us
    pallas_call x1, Pallas kernels, body(): pl.pallas_call(functools.partial(finish_kernel, lay), out_shape=[pltpu.HB...  1.35 us

profile of v4, /device:TPU:1, one launch (start us, length us, event | category | flops | bytes accessed | tf_op | source)
XLA Modules:
  0.0 34.9 jit_solution(11512268627481249801)
XLA Ops:
  0.6 32.9 %adjoint_step.1 = (f32[2048,128]{1,0:T(8,128)S(1)}, f32[2048,128]{1,0:T(8,128)S(1)}, f32[3,6,8,128]{3,2,1,0:T(8,128)S(1)}) custom-call(f32[2048,128]{1,0:T(8,128)} %bitcast.9, f32[2048,128]{1,0:T(8,128)} %bitcast.10, f32[3,2048,128]{2,1,0:T(8,128)} %bitcast.8, f32[2048,128]{1,0:T(8,128)} %bitcast.11, f32[2048,128]{1,0:T(8,128)} %bitcast.12, ...), custom_call_target="tpu_custom_call" | custom-call | tf_op jit(solution)/shard_map/adjoint_step/pallas_call | solution.py:896
  33.5 1.4 %finish.1 = (f32[2048,128]{1,0:T(8,128)}, f32[2048,128]{1,0:T(8,128)}) custom-call(f32[2048,128]{1,0:T(8,128)S(1)} %get-tuple-element.7.residual, f32[2048,128]{1,0:T(8,128)S(1)} %get-tuple-element.8.solved, f32[3,6,8,128]{3,2,1,0:T(8,128)S(1)} %get-tuple-element.9.grid), custom_call_target="tpu_custom_call" | custom-call | tf_op jit(solution)/shard_map/finish/pallas_call | solution.py:926
